TPU v7x, 256 devices: a whole 4x4x8 slice. The times are simulated.
256 devices in a mesh: role: 4 (over z_hi), dp: 8 (over x, core), mp: 8 (over y, z_lo).
Axes of the slice: x: 4, y: 4, z: 8 (z_hi: 4, z_lo: 2; z = z_hi * 2 + z_lo), core: 2. Of those that a mesh axis runs over, the one named last changes fastest.
Arguments:
- teacher_hidden: bfloat16 [8192, 2560], P('dp', ('role', 'mp')), may hold values from -20 to 20
- teacher_gain: float32 [2560], replicated, may hold values from 0.25 to 1.75
- teacher_head: bfloat16 [2560, 3, 8192], P(None, None, ('role', 'mp')), may hold values from -4.1504894 to 4.1504894
- student_hidden: bfloat16 [8192, 1024], P('dp', ('role', 'mp')), may hold values from -20 to 20
- norm_gain: float32 [1024], replicated, may hold values from 0.25 to 1.75
- gate_weight: bfloat16 [1024, 4096], P(None, ('role', 'mp')), may hold values from -0.1875 to 0.1875
- up_weight: bfloat16 [1024, 4096], P(None, ('role', 'mp')), may hold values from -0.1875 to 0.1875
- down_weight: bfloat16 [4096, 1024], P(('role', 'mp')), may hold values from -0.09375 to 0.09375
- final_gain: float32 [1024], replicated, may hold values from 0.25 to 1.75
- student_head: bfloat16 [1024, 3, 8192], P(None, None, ('role', 'mp')), may hold values from -6.5625 to 6.5625
- sampled_codes: int32 [8192], P('dp'), may hold values from 0 to 8191
- levels: int32 [8192], P('dp'), may hold values from 0 to 2
Outputs:
- token_kl: float32 [8192], P('dp')
- sampled_score: float32 [8192], P('dp')
- head_grad: float32 [1024, 3, 8192], P('dp', None, ('role', 'mp'))
- gate_grad: float32 [1024, 4096], P('dp', ('role', 'mp'))
- up_grad: float32 [1024, 4096], P('dp', ('role', 'mp'))
- down_grad: float32 [4096, 1024], P(('role', 'mp'), 'dp')
- input_grad: float32 [8192, 1024], P('dp', ('role', 'mp'))
All inputs are finite; a program needn't handle non-finite values.
Results may differ from a plain program's by a relative error of at most 0.035.
Values may be sent and summed in bfloat16 or wider, within the bound.
No kernel may reach another device: no remote copies, remote signals or barrier semaphores. Data moves between devices by JAX's collectives and lax.ppermute only.
A program may use at most 128 MiB of HBM per device.

v0:
```python
import jax
import jax.numpy as jnp
from jax import lax
from jax.sharding import PartitionSpec as P

NORM_EPS = 1e-06


def silu_parts(gate_pre):
    sigma = jax.nn.sigmoid(gate_pre)
    return (gate_pre * sigma, sigma * (1.0 + gate_pre * (1.0 - sigma)))


def body(
    teacher_hidden,
    teacher_gain,
    teacher_head,
    student_hidden,
    norm_gain,
    gate_weight,
    up_weight,
    down_weight,
    final_gain,
    student_head,
    sampled_codes,
    levels,
):
    row_count = teacher_hidden.shape[0]
    level_count = teacher_head.shape[1]
    code_count = teacher_head.shape[2]
    width_t = teacher_gain.shape[0]
    width_s = norm_gain.shape[0]
    width_share = student_hidden.shape[1]
    share_start = lax.axis_index(("role", "mp")) * width_share
    teacher_flat = teacher_head.reshape(width_t, level_count * code_count)
    student_flat = student_head.reshape(width_s, level_count * code_count)
    level_mask = (levels[:, None] == jnp.arange(level_count, dtype=jnp.int32)[None, :]).astype(
        jnp.float32
    )
    teacher_full, student_full = (
        lax.all_gather(teacher_hidden, ("role", "mp"), axis=1, tiled=True),
        lax.all_gather(student_hidden, ("role", "mp"), axis=1, tiled=True),
    )
    teacher_wide = teacher_full.astype(jnp.float32)
    teacher_scale = lax.rsqrt(jnp.mean(teacher_wide * teacher_wide, axis=1) + NORM_EPS)
    teacher_normed = (teacher_wide * teacher_scale[:, None] * teacher_gain).astype(jnp.bfloat16)
    teacher_all = jnp.dot(teacher_normed, teacher_flat, preferred_element_type=jnp.float32)
    teacher_logits = jnp.sum(
        teacher_all.reshape(row_count, level_count, code_count) * level_mask[:, :, None], axis=1
    )
    student_in = student_full.astype(jnp.float32)
    scale_in = lax.rsqrt(jnp.mean(student_in * student_in, axis=1) + NORM_EPS)
    normed_in = (student_in * scale_in[:, None] * norm_gain).astype(jnp.bfloat16)
    gate_pre = jnp.dot(normed_in, gate_weight, preferred_element_type=jnp.float32)
    up_pre = jnp.dot(normed_in, up_weight, preferred_element_type=jnp.float32)
    gate_act, gate_slope = silu_parts(gate_pre)
    hidden = (gate_act * up_pre).astype(jnp.bfloat16)
    down_part = jnp.dot(hidden, down_weight, preferred_element_type=jnp.float32)
    mixed_rows = student_in + lax.psum(down_part, ("role", "mp"))
    scale_out = lax.rsqrt(jnp.mean(mixed_rows * mixed_rows, axis=1) + NORM_EPS)
    normed_out = (mixed_rows * scale_out[:, None] * final_gain).astype(jnp.bfloat16)
    student_all = jnp.dot(normed_out, student_flat, preferred_element_type=jnp.float32)
    student_logits = jnp.sum(
        student_all.reshape(row_count, level_count, code_count) * level_mask[:, :, None], axis=1
    )
    code_start = lax.axis_index(("role", "mp")) * code_count
    code_hit = (
        sampled_codes[:, None] == code_start + jnp.arange(code_count, dtype=jnp.int32)[None, :]
    ).astype(jnp.float32)
    local_score = jnp.sum(code_hit * teacher_logits, axis=1)
    peak_s, peak_t = lax.pmax(
        (jnp.max(student_logits, axis=1), jnp.max(teacher_logits, axis=1)), ("role", "mp")
    )
    expo_s = jnp.exp(student_logits - peak_s[:, None])
    expo_t = jnp.exp(teacher_logits - peak_t[:, None])
    total_s, total_t, cross_sum, score_sum = lax.psum(
        (
            jnp.sum(expo_s, axis=1),
            jnp.sum(expo_t, axis=1),
            jnp.sum(expo_t * (teacher_logits - student_logits), axis=1),
            local_score,
        ),
        ("role", "mp"),
    )
    norm_s = peak_s + jnp.log(total_s)
    norm_t = peak_t + jnp.log(total_t)
    token_kl = cross_sum / total_t - norm_t + norm_s
    sampled_score = score_sum - norm_t
    code_grad = jnp.exp(student_logits - norm_s[:, None]) - jnp.exp(
        teacher_logits - norm_t[:, None]
    )
    grad_full = (
        (level_mask[:, :, None] * code_grad[:, None, :])
        .astype(jnp.bfloat16)
        .reshape(row_count, level_count * code_count)
    )
    code_part = lax.dot_general(
        grad_full, student_flat, (((1,), (1,)), ((), ())), preferred_element_type=jnp.float32
    )
    back_out = lax.psum(code_part, ("role", "mp"))
    gained = final_gain * back_out
    back_mixed = (
        scale_out[:, None] * gained
        - mixed_rows * (scale_out**3)[:, None] * jnp.mean(gained * mixed_rows, axis=1)[:, None]
    )
    back_mixed_b = back_mixed.astype(jnp.bfloat16)
    back_own = lax.dynamic_slice_in_dim(back_mixed, share_start, width_share, 1)
    back_hidden = lax.dot_general(
        back_mixed_b, down_weight, (((1,), (1,)), ((), ())), preferred_element_type=jnp.float32
    )
    back_gate = (back_hidden * up_pre * gate_slope).astype(jnp.bfloat16)
    back_up = (back_hidden * gate_act).astype(jnp.bfloat16)
    over_rows = (((0,), (0,)), ((), ()))
    head_term = lax.dot_general(
        normed_out, grad_full, over_rows, preferred_element_type=jnp.float32
    )
    gate_term = lax.dot_general(normed_in, back_gate, over_rows, preferred_element_type=jnp.float32)
    up_term = lax.dot_general(normed_in, back_up, over_rows, preferred_element_type=jnp.float32)
    down_term = lax.dot_general(back_mixed_b, hidden, over_rows, preferred_element_type=jnp.float32)
    head_share, gate_share, up_share, down_share = (
        lax.psum_scatter(
            head_term.astype(jnp.bfloat16), "dp", scatter_dimension=0, tiled=True
        ).astype(jnp.float32),
        lax.psum_scatter(
            gate_term.astype(jnp.bfloat16), "dp", scatter_dimension=0, tiled=True
        ).astype(jnp.float32),
        lax.psum_scatter(
            up_term.astype(jnp.bfloat16), "dp", scatter_dimension=0, tiled=True
        ).astype(jnp.float32),
        lax.psum_scatter(
            down_term.astype(jnp.bfloat16), "dp", scatter_dimension=0, tiled=True
        ).astype(jnp.float32),
    )
    back_part = lax.dot_general(
        back_gate, gate_weight, (((1,), (1,)), ((), ())), preferred_element_type=jnp.float32
    )
    back_part = back_part + lax.dot_general(
        back_up, up_weight, (((1,), (1,)), ((), ())), preferred_element_type=jnp.float32
    )
    back_in = lax.psum(back_part.astype(jnp.bfloat16), ("role", "mp")).astype(jnp.float32)
    gained_in = norm_gain * back_in
    norm_part = (
        scale_in[:, None] * gained_in
        - student_in * (scale_in**3)[:, None] * jnp.mean(gained_in * student_in, axis=1)[:, None]
    )
    input_grad = back_own + lax.dynamic_slice_in_dim(norm_part, share_start, width_share, 1)
    head_grad = head_share.reshape(head_share.shape[0], level_count, code_count)
    return (token_kl, sampled_score, head_grad, gate_share, up_share, down_share.T, input_grad)


def solution(mesh):
    placed = (
        P("dp", ("role", "mp")),
        P(),
        P(None, None, ("role", "mp")),
        P("dp", ("role", "mp")),
        P(),
        P(None, ("role", "mp")),
        P(None, ("role", "mp")),
        P(("role", "mp"), None),
        P(),
        P(None, None, ("role", "mp")),
        P("dp"),
        P("dp"),
    )
    return jax.shard_map(
        body,
        mesh=mesh,
        in_specs=placed,
        out_specs=(
            P("dp"),
            P("dp"),
            P("dp", None, ("role", "mp")),
            P("dp", ("role", "mp")),
            P("dp", ("role", "mp")),
            P(("role", "mp"), "dp"),
            P("dp", ("role", "mp")),
        ),
        check_vma=False,
    )
```

profile of v0, /device:TPU:2, one launch (start us, length us, event | category | flops | bytes accessed | tf_op | source)
XLA Modules:
  0.0 1185.4 jit_solution(10532169492132673438)
XLA Ops:
  8.0 149.2 %all-gather.5.cloned.1.call-done = bf16[1024,1024]{0,1:T(8,128)(2,1)} async-done(((bf16[1024,32]{0,1:T(8,128)(2,1)}), bf16[1024,1024]{0,1:T(8,128)(2,1)}) %all-gather.5.cloned.1.call-update) | async-done | bytes 2097168 | tf_op jit(solution)/shard_map/all_gather | solution.py:42
  157.1 2.9 copy.35
  164.7 2.8 fusion.31
  168.4 2.6 copy.36
  171.0 6.4 copy.33
  177.5 151.3 %all-reduce.6.cloned.1.call-done = f32[1024,1024]{1,0:T(8,128)} async-done(((f32[1024,1024]{1,0:T(8,128)}), f32[1024,1024]{1,0:T(8,128)}) %all-reduce.6.cloned.1.call-update) | async-done | bytes 4194320 | tf_op jit(solution)/shard_map/psum | solution.py:59
  328.8 2.9 multiply_reduce_fusion.2
  336.3 143.2 %all-gather.3.cloned.1.call-done = bf16[1024,2560]{0,1:T(8,128)(2,1)} async-done(((bf16[1024,80]{0,1:T(8,128)(2,1)}), bf16[1024,2560]{0,1:T(8,128)(2,1)}) %all-gather.3.cloned.1.call-update) | async-done | bytes 5242896 | tf_op jit(solution)/shard_map/all_gather | solution.py:41
  479.5 3.8 fusion
  483.5 8.1 multiply_reduce_fusion.5
  493.1 74.8 %all-reduce.1 = (f32[1024]{0:T(1024)S(1)}, f32[1024]{0:T(1024)S(1)}) all-reduce(f32[1024]{0:T(1024)S(1)} %reduce_max.18, f32[1024]{0:T(1024)S(1)} %reduce_max.19), channel_id=1, replica_groups=mesh['role'=4,'dp'=8,'mp'=8] {'role','mp'}, use_global_device_ids=true, to_apply=%region_3.0 | all-reduce | flops 2048 | bytes 16384 | tf_op jit(solution)/shard_map/pmax | solution.py:71
  570.4 137.9 %all-reduce = (f32[1024]{0:T(1024)S(1)}, f32[1024]{0:T(1024)S(1)}, f32[1024]{0:T(1024)S(1)}, f32[1024]{0:T(1024)S(1)}) all-reduce(f32[1024]{0:T(1024)S(1)} %get-tuple-element.29, f32[1024]{0:T(1024)S(1)} %get-tuple-element.31, f32[1024]{0:T(1024)S(1)} %get-tuple-element.28, ...), channel_id=1, replica_groups=mesh['role'=4,'dp'=8,'mp'=8] {'role','mp'}, use_global_device_ids=true, to_apply=%region_11.0 | all-reduce | flops 4096 | bytes 32768 | tf_op jit(solution)/shard_map/psum | solution.py:76
  712.0 5.3 convolution_bitcast_fusion
  720.2 2.6 copy.37
  722.8 5.1 convolution_convert_fusion
  727.9 150.3 %all-reduce.8.cloned.1.call-done = f32[1024,1024]{1,0:T(8,128)} async-done(((f32[1024,1024]{1,0:T(8,128)}), f32[1024,1024]{1,0:T(8,128)}) %all-reduce.8.cloned.1.call-update) | async-done | bytes 4194320 | tf_op jit(solution)/shard_map/psum | solution.py:100
  878.2 4.3 multiply_reduce_fusion.1
  888.9 3.2 multiply_convert_fusion.3
  893.7 3.1 convolution_convert_fusion.3
  902.4 7.5 reduce-scatter.5.cloned.1.call-done
  911.9 32.5 %reduce-scatter.11.cloned.1.call-done = bf16[128,128]{1,0:T(8,128)(2,1)} async-done(((bf16[1024,128]{1,0:T(8,128)(2,1)}), bf16[128,128]{1,0:T(8,128)(2,1)}) %reduce-scatter.11.cloned.1.call-update) | async-done | bytes 32784 | tf_op jit(solution)/shard_map/reduce_scatter | solution.py:130
  945.9 33.1 %reduce-scatter.9.cloned.1.call-done = bf16[128,128]{1,0:T(8,128)(2,1)} async-done(((bf16[1024,128]{1,0:T(8,128)(2,1)}), bf16[128,128]{1,0:T(8,128)(2,1)}) %reduce-scatter.9.cloned.1.call-update) | async-done | bytes 32784 | tf_op jit(solution)/shard_map/reduce_scatter | solution.py:127
  980.4 33.0 %reduce-scatter.7.cloned.1.call-done = bf16[128,128]{1,0:T(8,128)(2,1)} async-done(((bf16[1024,128]{1,0:T(8,128)(2,1)}), bf16[128,128]{1,0:T(8,128)(2,1)}) %reduce-scatter.7.cloned.1.call-update) | async-done | bytes 32784 | tf_op jit(solution)/shard_map/reduce_scatter | solution.py:124
  1014.8 158.7 %all-reduce.10.cloned.1.call-done = bf16[1024,1024]{1,0:T(8,128)(2,1)} async-done(((bf16[1024,1024]{1,0:T(8,128)(2,1)}), bf16[1024,1024]{1,0:T(8,128)(2,1)}) %all-reduce.10.cloned.1.call-update) | async-done | bytes 2097168 | tf_op jit(solution)/shard_map/psum | solution.py:140
  (103 shorter events, 46.5 us)
Async XLA Ops:
  7.2 157.5 %copy-start = (bf16[128,1024]{1,0:T(8,128)(2,1)S(1)}, bf16[128,1024]{1,0:T(8,128)(2,1)}, u32[]{:S(2)}) copy-start(bf16[128,1024]{1,0:T(8,128)(2,1)} %param.19) | copy-start | bytes 786436
  7.2 153.3 %copy-start.21 = (f32[1024]{0:T(1024)S(1)}, f32[1024]{0:T(1024)}, u32[]{:S(2)}) copy-start(f32[1024]{0:T(1024)} %param.16) | copy-start | bytes 12292
  7.2 149.9 %all-gather.5.cloned.1.call-start = ((), (), s32[]{:S(2)}) async-start(), calls=%async_computation.5 | async-start | bytes 2162688 | tf_op jit(solution)/shard_map/all_gather | solution.py:42
  7.9 320.8 %all-reduce.6.cloned.1.call-start = ((), (), s32[]{:S(2)}) async-start(), calls=%async_computation.6 | async-start | bytes 8388608 | tf_op jit(solution)/shard_map/psum | solution.py:59
  160.0 2.4 copy-start.18
  167.4 312.0 %all-gather.3.cloned.1.call-start = ((), (), s32[]{:S(2)}) async-start(), calls=%async_computation.4 | async-start | bytes 5406720 | tf_op jit(solution)/shard_map/all_gather | solution.py:41
  168.2 710.1 %all-reduce.8.cloned.1.call-start = ((), (), s32[]{:S(2)}) async-start(), calls=%async_computation.8 | async-start | bytes 8388608 | tf_op jit(solution)/shard_map/psum | solution.py:100
  171.0 6.4 copy-start.23
  177.4 154.3 %copy-start.20 = (f32[1024]{0:T(1024)S(1)}, f32[1024]{0:T(1024)}, u32[]{:S(2)}) copy-start(f32[1024]{0:T(1024)} %param.20) | copy-start | bytes 12292
  328.7 3.4 copy-start.1
  336.1 147.2 %copy-start.24 = (f32[2560]{0:T(1024)S(1)}, f32[2560]{0:T(1024)}, u32[]{:S(2)}) copy-start(f32[2560]{0:T(1024)} %param.13) | copy-start | bytes 30724
  479.5 4.0 copy-start.7
  483.5 84.4 %copy-start.22 = (s32[1024]{0:T(1024)S(1)}, s32[1024]{0:T(1024)}, u32[]{:S(2)}) copy-start(s32[1024]{0:T(1024)} %param.22) | copy-start | bytes 12292
  717.4 192.5 %reduce-scatter.5.cloned.1.call-start = ((), (), s32[]{:S(2)}) async-start(), calls=%async_computation.7 | async-start | bytes 1769472 | tf_op jit(solution)/shard_map/reduce_scatter | solution.py:121
  727.9 216.6 %reduce-scatter.11.cloned.1.call-start = ((), (), s32[]{:S(2)}) async-start(), calls=%async_computation.11 | async-start | bytes 294912 | tf_op jit(solution)/shard_map/reduce_scatter | solution.py:130
  878.2 4.6 copy-start.2
  878.2 5.9 copy-start.6
  884.2 3.2 copy-start.15
  888.9 90.2 %reduce-scatter.9.cloned.1.call-start = ((), (), s32[]{:S(2)}) async-start(), calls=%async_computation.10 | async-start | bytes 294912 | tf_op jit(solution)/shard_map/reduce_scatter | solution.py:127
  888.9 3.2 copy-start.4
  892.1 5.1 copy-start.17
  893.7 119.7 %reduce-scatter.7.cloned.1.call-start = ((), (), s32[]{:S(2)}) async-start(), calls=%async_computation.9 | async-start | bytes 294912 | tf_op jit(solution)/shard_map/reduce_scatter | solution.py:124
  893.7 4.2 copy-start.19
  896.9 276.6 %all-reduce.10.cloned.1.call-start = ((), (), s32[]{:S(2)}) async-start(), calls=%async_computation.12 | async-start | bytes 4194304 | tf_op jit(solution)/shard_map/psum | solution.py:140
  (10 other events, 13.7 us)
Sparse Core Ops, SparseCore 0:
  9.8 147.2 all-gather.4
  167.6 161.1 all-reduce.5
  330.7 148.7 all-gather.2
  717.5 160.6 all-reduce.7
  880.6 29.2 reduce-scatter.4
  912.3 32.1 reduce-scatter.10
  947.1 31.8 reduce-scatter.8
  981.5 31.8 reduce-scatter.6
  1017.4 156.1 all-reduce.9
where the time goes:
time: 1190 us
  waiting for transfers between devices  860 us (72%)
  blocking collectives  213 us (18%)
  matrix products  37.4 us (3%)
  other arithmetic  32.9 us (3%)
  local copies, waits for them, and re-layouts  27 us (2%)
  between operations  14.2 us (1%)
    psum x1, waiting for transfers between devices, body(): lax.psum(back_part.astype(jnp.bfloat16), ('role', 'mp')).astype(jnp.float32)  159 us
    psum x1, waiting for transfers between devices, body(): mixed_rows = student_in + lax.psum(down_part, ('role', 'mp'))  151 us
    psum x1, waiting for transfers between devices, body(): back_out = lax.psum(code_part, ('role', 'mp'))  150 us
    all_gather x1, waiting for transfers between devices, body(): lax.all_gather(student_hidden, ('role', 'mp'), axis=1, tiled=True)  149 us
    all_gather x1, waiting for transfers between devices, body(): lax.all_gather(teacher_hidden, ('role', 'mp'), axis=1, tiled=True)  143 us
    psum x1, blocking collectives, body(): lax.psum((jnp.sum(expo_s, axis=1), jnp.sum(expo_t, axis=1), jnp.sum(expo_...  138 us
    pmax x1, blocking collectives, body(): lax.pmax((jnp.max(student_logits, axis=1), jnp.max(teacher_logits, axis=1...  74.8 us
    reduce_scatter x1, waiting for transfers between devices, body(): lax.psum_scatter(up_term.astype(jnp.bfloat16), 'dp', scatter_dimension=0,...  33.1 us
  transfers between devices with their start and end apart: 9, of which 9 were waited for; matrix products, arithmetic and copies ran while one was open for 4% of the time, Pallas kernels for 0%

commit v1 on v0

v1 whole, which is shorter than its diff:
```python
import jax
import jax.numpy as jnp
from jax import lax
from jax.sharding import Mesh, PartitionSpec as P

NORM_EPS = 1e-06
OUTER = "zh"
INNER = ("y", "zl")
GROUP = ("zh", "y", "zl")
ROWS = ("x", "core")
F32 = jnp.float32
BF16 = jnp.bfloat16


def dot(a, b, da, db):
    return lax.dot_general(a, b, (((da,), (db,)), ((), ())), preferred_element_type=F32)


def spread(block, axes, count):
    copies = jnp.broadcast_to(block[None], (count,) + block.shape)
    got = lax.all_to_all(copies, axes, 0, 0, tiled=True)
    return got.reshape((count * block.shape[0],) + block.shape[1:])


def collect(terms, axes, count):
    parts = terms.reshape((count, terms.shape[0] // count) + terms.shape[1:])
    got = lax.all_to_all(parts, axes, 0, 0, tiled=True)
    return jnp.sum(got.astype(F32), axis=0)


def body(
    teacher_hidden,
    teacher_gain,
    teacher_head,
    student_hidden,
    norm_gain,
    gate_weight,
    up_weight,
    down_weight,
    final_gain,
    student_head,
    sampled_codes,
    levels,
):
    outer, inner, dp = 4, 8, 8
    row_count = teacher_hidden.shape[0]
    level_count = teacher_head.shape[1]
    code_count = teacher_head.shape[2]
    width_t = teacher_gain.shape[0]
    width_s = norm_gain.shape[0]
    share = student_hidden.shape[1]
    outer_at = lax.axis_index(OUTER)
    inner_at = lax.axis_index(INNER)
    group_at = outer_at * inner + inner_at

    def to_gathered(w):
        return jnp.swapaxes(w.reshape((outer, inner, -1) + w.shape[1:]), 0, 1).reshape(w.shape)

    def from_gathered(w):
        return jnp.swapaxes(w.reshape((inner, outer, -1) + w.shape[1:]), 0, 1).reshape(w.shape)

    teacher_flat = teacher_head.reshape(width_t, level_count * code_count)
    student_flat = student_head.reshape(width_s, level_count * code_count)
    level_mask = (jnp.arange(level_count, dtype=jnp.int32)[:, None] == levels[None, :]).astype(F32)

    teacher_t = lax.all_gather(teacher_hidden.T, OUTER, axis=0, tiled=True)
    teacher_t = lax.all_gather(teacher_t, INNER, axis=0, tiled=True)

    own_cols = student_hidden.T
    student_t = spread(spread(own_cols, OUTER, outer), INNER, inner)
    student_in = student_t.astype(F32)
    scale_in = lax.rsqrt(jnp.mean(student_in * student_in, axis=0) + NORM_EPS)
    gain_in = to_gathered(norm_gain)
    normed_in = (student_in * scale_in[None, :] * gain_in[:, None]).astype(BF16)
    both_weight = to_gathered(jnp.concatenate([gate_weight, up_weight], axis=1))
    both_pre = dot(both_weight, normed_in, 0, 0)
    units = gate_weight.shape[1]
    gate_pre, up_pre = both_pre[:units], both_pre[units:]
    sigma = jax.nn.sigmoid(gate_pre)
    gate_act = gate_pre * sigma
    gate_slope = sigma * (1.0 + gate_pre * (1.0 - sigma))
    hidden = (gate_act * up_pre).astype(BF16)
    down_part = dot(hidden, down_weight, 0, 0).astype(BF16)
    down_own = collect(collect(down_part, INNER, inner).astype(BF16), OUTER, outer)
    own_rows = row_count // (outer * inner)
    row_start = (inner_at * outer + outer_at) * own_rows
    student_own = lax.dynamic_slice_in_dim(student_t, row_start, own_rows, 1).astype(F32)
    mixed_rows = from_gathered(student_own).T + down_own
    scale_out = lax.rsqrt(jnp.mean(mixed_rows * mixed_rows, axis=1) + NORM_EPS)
    normed_own = (mixed_rows * scale_out[:, None] * final_gain).astype(BF16)
    normed_out = spread(spread(normed_own, OUTER, outer), INNER, inner)

    teacher_wide = from_gathered(teacher_t).astype(F32)
    teacher_scale = lax.rsqrt(jnp.mean(teacher_wide * teacher_wide, axis=0) + NORM_EPS)
    teacher_normed = (teacher_wide * teacher_scale[None, :] * teacher_gain[:, None]).astype(BF16)

    def pick_level(all_levels):
        return jnp.sum(
            all_levels.reshape(level_count, code_count, row_count) * level_mask[:, None, :], axis=0
        )

    teacher_logits = pick_level(dot(teacher_flat, teacher_normed, 0, 0))
    student_logits = pick_level(dot(student_flat, normed_out, 0, 1))
    peak_s = jnp.max(student_logits, axis=0)
    peak_t = jnp.max(teacher_logits, axis=0)
    expo_t = jnp.exp(teacher_logits - peak_t)
    total_t = jnp.sum(expo_t, axis=0)
    part_s = peak_s + jnp.log(jnp.sum(jnp.exp(student_logits - peak_s), axis=0))
    part_t = peak_t + jnp.log(total_t)
    part_cross = jnp.sum(expo_t * (teacher_logits - student_logits), axis=0) / total_t
    codes_here = group_at * code_count + jnp.arange(code_count, dtype=jnp.int32)
    part_score = jnp.sum(
        jnp.where(codes_here[:, None] == sampled_codes[None, :], teacher_logits, 0.0), axis=0
    )
    stats = jnp.stack([part_s, part_t, part_cross, part_score])
    stats = spread(stats, GROUP, outer * inner).reshape(outer * inner, 4, row_count)
    norm_s = jax.nn.logsumexp(stats[:, 0], axis=0)
    norm_t = jax.nn.logsumexp(stats[:, 1], axis=0)
    cross = jnp.sum(jnp.exp(stats[:, 1] - norm_t) * stats[:, 2], axis=0)
    token_kl = cross - norm_t + norm_s
    sampled_score = jnp.sum(stats[:, 3], axis=0) - norm_t
    code_grad = jnp.exp(student_logits - norm_s) - jnp.exp(teacher_logits - norm_t)
    grad_full = (
        (level_mask[:, None, :] * code_grad[None])
        .astype(BF16)
        .reshape(level_count * code_count, row_count)
    )

    code_part = dot(grad_full, student_flat, 0, 1)
    back_out = collect(collect(code_part, INNER, inner), OUTER, outer)
    head_term = dot(normed_out, grad_full, 0, 1).astype(BF16)
    head_share = lax.psum_scatter(head_term, ROWS, scatter_dimension=0, tiled=True).astype(F32)
    gained = final_gain * back_out
    back_mixed = (
        scale_out[:, None] * gained
        - mixed_rows * (scale_out**3)[:, None] * jnp.mean(gained * mixed_rows, axis=1)[:, None]
    )
    back_mixed_b = spread(spread(back_mixed.astype(BF16), OUTER, outer), INNER, inner)

    back_hidden = dot(down_weight, back_mixed_b, 1, 1)
    back_both = jnp.concatenate(
        [
            (back_hidden * up_pre * gate_slope).astype(BF16),
            (back_hidden * gate_act).astype(BF16),
        ]
    )
    both_term = from_gathered(dot(normed_in, back_both, 1, 1).astype(BF16))
    down_term = dot(back_mixed_b, hidden, 0, 1).astype(BF16)
    grad_share = lax.psum_scatter(
        jnp.concatenate([both_term, down_term], axis=1), ROWS, scatter_dimension=0, tiled=True
    ).astype(F32)
    gate_share = grad_share[:, :units]
    up_share = grad_share[:, units : 2 * units]
    down_share = grad_share[:, 2 * units :].T

    back_part = dot(both_weight, back_both, 1, 0)
    row_part = jnp.sum(gain_in[:, None] * student_in * back_part, axis=0)

    def with_rows(part, row_term, count):
        high = row_term.astype(BF16)
        low = (row_term - high.astype(F32)).astype(BF16)
        extra = jnp.concatenate(
            [high[None], low[None], jnp.zeros((14, row_count), BF16)], axis=0
        )
        part = part.astype(BF16).reshape(count, -1, row_count)
        extra = jnp.broadcast_to(extra[None], (count, 16, row_count))
        return jnp.concatenate([part, extra], axis=1).reshape(-1, row_count)

    got = collect(with_rows(back_part, row_part, inner), INNER, inner)
    block = outer * share
    got = collect(with_rows(got[:block], got[block] + got[block + 1], outer), OUTER, outer)
    back_in = got[:share]
    row_mean = (got[share] + got[share + 1]) / width_s
    share_start = group_at * share
    back_own = lax.dynamic_slice_in_dim(back_mixed_b, share_start, share, 1).T.astype(F32)
    own_gain = lax.dynamic_slice_in_dim(norm_gain, share_start, share, 0)
    input_grad = (
        back_own
        + scale_in * own_gain[:, None] * back_in
        - own_cols.astype(F32) * (scale_in**3 * row_mean)
    ).T
    head_grad = head_share.reshape(head_share.shape[0], level_count, code_count)
    return (token_kl, sampled_score, head_grad, gate_share, up_share, down_share, input_grad)


def solution(mesh):
    split = Mesh(mesh.devices.reshape(4, 4, 2, 4, 2), ("zh", "x", "core", "y", "zl"))
    placed = (
        P(ROWS, GROUP),
        P(),
        P(None, None, GROUP),
        P(ROWS, GROUP),
        P(),
        P(None, GROUP),
        P(None, GROUP),
        P(GROUP, None),
        P(),
        P(None, None, GROUP),
        P(ROWS),
        P(ROWS),
    )
    return jax.shard_map(
        body,
        mesh=split,
        in_specs=placed,
        out_specs=(
            P(ROWS),
            P(ROWS),
            P(ROWS, None, GROUP),
            P(ROWS, GROUP),
            P(ROWS, GROUP),
            P(GROUP, ROWS),
            P(ROWS, GROUP),
        ),
        check_vma=False,
    )
```

time: 1190 us -> 511 us (0.43)
  waiting for transfers between devices: 860 us -> 140 us
  starting transfers between devices: 0.81 us -> 28.7 us
  blocking collectives: 213 us -> 233 us
  matrix products: 37.4 us -> 24.8 us
    psum x3 -> x0, waiting for transfers between devices: 460 us -> none  [the longest x1 159 us: body(): lax.psum(back_part.astype(jnp.bfloat16), ('role', 'mp')).astype(jnp.float32)]
    all_gather x2 -> x1, waiting for transfers between devices: 292 us -> 53 us  [body(): teacher_t = lax.all_gather(teacher_t, INNER, axis=0, tiled=True)]
    all_to_all x0 -> x7, blocking collectives: none -> 195 us  [the longest x3 123 us: collect(): got = lax.all_to_all(parts, axes, 0, 0, tiled=True)]
    psum x1 -> x0, blocking collectives: 138 us -> none  [body(): lax.psum((jnp.sum(expo_s, axis=1), jnp.sum(expo_t, axis=1), jnp.sum(expo_...]
    pmax x1 -> x0, blocking collectives: 74.8 us -> none  [body(): lax.pmax((jnp.max(student_logits, axis=1), jnp.max(teacher_logits, axis=1...]
    reduce_scatter x4 -> x2, waiting for transfers between devices: 106 us -> 32 us  [the longest x1 32 us: body(): lax.psum_scatter(jnp.concatenate([both_term, down_term], axis=1), ROWS, s...]
    all_to_all x0 -> x6, waiting for transfers between devices: none -> 54.7 us  [the longest x3 30.4 us: collect(): got = lax.all_to_all(parts, axes, 0, 0, tiled=True)]
    all_gather x0 -> x1, blocking collectives: none -> 37.6 us  [body(): teacher_t = lax.all_gather(teacher_hidden.T, OUTER, axis=0, tiled=True)]
  transfers between devices with their start and end apart: 9 -> 9, of which waited for: 9 -> 5; matrix products, arithmetic and copies ran while one was open for 4% -> 9% of each run, Pallas kernels for 0% -> 0%
where the time goes in v1:
time: 511 us; the launch traced here: 506 us
  blocking collectives  233 us (46%)
  waiting for transfers between devices  140 us (27%)
  local copies, waits for them, and re-layouts  34.4 us (7%)
  other arithmetic  31.4 us (6%)
  starting transfers between devices  28.7 us (6%)
  matrix products  24.8 us (5%)
  between operations  14.4 us (3%)
    all_to_all x3, blocking collectives, collect(): got = lax.all_to_all(parts, axes, 0, 0, tiled=True)  123 us
    all_to_all x4, blocking collectives, spread(): got = lax.all_to_all(copies, axes, 0, 0, tiled=True)  72.3 us
    all_gather x1, waiting for transfers between devices, body(): teacher_t = lax.all_gather(teacher_t, INNER, axis=0, tiled=True)  53 us
    all_gather x1, blocking collectives, body(): teacher_t = lax.all_gather(teacher_hidden.T, OUTER, axis=0, tiled=True)  37.6 us
    reduce_scatter x1, waiting for transfers between devices, body(): lax.psum_scatter(jnp.concatenate([both_term, down_term], axis=1), ROWS, s...  32 us
    all_to_all x3, waiting for transfers between devices, collect(): got = lax.all_to_all(parts, axes, 0, 0, tiled=True)  30.4 us
    dot_general x10, matrix products, dot(): lax.dot_general(a, b, (((da,), (db,)), ((), ())), preferred_element_type=...  24.8 us
    all_to_all x3, waiting for transfers between devices, spread(): got = lax.all_to_all(copies, axes, 0, 0, tiled=True)  24.3 us
  transfers between devices with their start and end apart: 9, of which 5 were waited for; matrix products, arithmetic and copies ran while one was open for 9% of the time, Pallas kernels for 0%

profile of v1, /device:TPU:2, one launch (start us, length us, event | category | flops | bytes accessed | tf_op | source)
XLA Modules:
  0.0 505.9 jit_solution(8571136935606401940)
XLA Ops:
  8.1 19.3 %all_to_all.65 = bf16[4,32,1024]{2,1,0:T(8,128)(2,1)S(1)} all-to-all(bf16[4,32,1024]{2,1,0:T(8,128)(2,1)S(1)} %broadcast_in_dim.27), channel_id=1, replica_groups=mesh['zh'=4,'x'=4,'core'=2,'y'=4,'zl'=2] {'zh'}, dimensions={0} | all-to-all | bytes 524288 | tf_op jit(solution)/shard_map/all_to_all | solution.py:21
  29.1 5.0 all-to-all-start.1
  34.1 37.6 %all_gather.6 = bf16[320,1024]{1,0:T(8,128)(2,1)} all-gather(bf16[80,1024]{1,0:T(8,128)(2,1)S(1)} %bitcast.140), channel_id=1, replica_groups=mesh['zh'=4,'x'=4,'core'=2,'y'=4,'zl'=2] {'zh'}, dimensions={0}, use_global_device_ids=true | all-gather | bytes 819200 | tf_op jit(solution)/shard_map/all_gather | solution.py:66
  76.5 51.9 %all_to_all.66 = bf16[8,128,1024]{2,1,0:T(8,128)(2,1)} all-to-all(bf16[8,128,1024]{2,1,0:T(8,128)(2,1)S(1)} %bitcast.115), channel_id=1, replica_groups=mesh['zh'=4,'x'=4,'core'=2,'y'=4,'zl'=2] {'y','zl'}, dimensions={0} | all-to-all | bytes 4194304 | tf_op jit(solution)/shard_map/all_to_all | solution.py:27
  131.1 4.0 all-to-all-start.3
  136.0 11.7 %all-to-all-done.3 = bf16[4,32,1024]{2,1,0:T(8,128)(2,1)S(1)} async-done(((bf16[4,32,1024]{2,1,0:T(8,128)(2,1)}), bf16[4,32,1024]{2,1,0:T(8,128)(2,1)S(1)}, u32[]{:S(2)}, u32[]{:S(2)}) %all-to-all-start.3) | async-done | bytes 262176 | tf_op jit(solution)/shard_map/all_to_all | solution.py:27
  148.9 16.3 %all_to_all.67 = bf16[4,32,1024]{2,1,0:T(8,128)(2,1)S(1)} all-to-all(bf16[4,32,1024]{2,1,0:T(8,128)(2,1)S(1)} %broadcast_in_dim.31), channel_id=1, replica_groups=mesh['zh'=4,'x'=4,'core'=2,'y'=4,'zl'=2] {'zh'}, dimensions={0} | all-to-all | bytes 524288 | tf_op jit(solution)/shard_map/all_to_all | solution.py:21
  166.9 4.6 all-to-all-start.5
  174.2 6.1 %copy.160 = bf16[2560,3,256]{0,2,1:T(8,128)(2,1)} copy(bf16[2560,3,256]{2,0,1:T(8,128)(2,1)} %param.14) | data formatting | bytes 7864320 | tf_op args[2]
  180.9 53.0 %all-gather.2.cloned.1.call-done = bf16[2560,1024]{1,0:T(8,128)(2,1)} async-done(((bf16[320,1024]{1,0:T(8,128)(2,1)}), bf16[2560,1024]{1,0:T(8,128)(2,1)}) %all-gather.2.cloned.1.call-update) | async-done | bytes 5242896 | tf_op jit(solution)/shard_map/all_gather | solution.py:67
  241.3 5.9 %fusion.39 = f32[1024,768]{0,1:T(8,128)} fusion(bf16[2560,768]{0,1:T(8,128)(2,1)S(1)} %bitcast.119, bf16[2560,1024]{1,0:T(8,128)(2,1)S(1)} %bitcast.118), kind=kOutput, calls=%fused_computation.105 | convolution fusion | flops 4026531840 | bytes 12320768 | tf_op jit(solution)/shard_map/dot_general | solution.py:16
  247.3 4.0 fusion.37
  258.5 24.5 %all_to_all.68 = f32[32,4,1024]{2,1,0:T(4,128)S(1)} all-to-all(f32[32,4,1024]{2,1,0:T(4,128)S(1)} %broadcast_in_dim.35), channel_id=1, replica_groups=mesh['zh'=4,'x'=4,'core'=2,'y'=4,'zl'=2] {'zh','y','zl'}, dimensions={0} | all-to-all | bytes 1048576 | tf_op jit(solution)/shard_map/all_to_all | solution.py:21
  293.0 53.5 %all_to_all.69 = f32[8,128,1024]{2,1,0:T(8,128)} all-to-all(f32[8,128,1024]{2,1,0:T(8,128)S(1)} %fusion.38), channel_id=1, replica_groups=mesh['zh'=4,'x'=4,'core'=2,'y'=4,'zl'=2] {'y','zl'}, dimensions={0} | all-to-all | bytes 8388608 | tf_op jit(solution)/shard_map/all_to_all | solution.py:27
  349.1 17.2 %all_to_all.70 = f32[4,32,1024]{2,1,0:T(8,128)S(1)} all-to-all(f32[4,32,1024]{2,1,0:T(8,128)S(1)} %bitcast.126), channel_id=1, replica_groups=mesh['zh'=4,'x'=4,'core'=2,'y'=4,'zl'=2] {'zh'}, dimensions={0} | all-to-all | bytes 1048576 | tf_op jit(solution)/shard_map/all_to_all | solution.py:27
  366.6 12.2 %all_to_all.71 = bf16[4,32,1024]{2,1,0:T(8,128)(2,1)S(1)} all-to-all(bf16[4,32,1024]{2,1,0:T(8,128)(2,1)S(1)} %broadcast_in_dim.36), channel_id=1, replica_groups=mesh['zh'=4,'x'=4,'core'=2,'y'=4,'zl'=2] {'zh'}, dimensions={0} | all-to-all | bytes 524288 | tf_op jit(solution)/shard_map/all_to_all | solution.py:21
  380.6 4.5 all-to-all-start.10
  385.3 24.3 %all-to-all-done.10 = bf16[8,128,1024]{1,2,0:T(8,128)(2,1)} async-done(((bf16[8,128,1024]{1,2,0:T(8,128)(2,1)}), bf16[8,128,1024]{1,2,0:T(8,128)(2,1)}, u32[]{:S(2)}, u32[]{:S(2)}) %all-to-all-start.10) | async-done | bytes 2097184 | tf_op jit(solution)/shard_map/all_to_all | solution.py:21
  409.6 3.9 copy.169
  418.7 4.4 all-to-all-start.11
  423.2 5.1 %convolution_convert_fusion.1 = bf16[1024,768]{1,0:T(8,128)(2,1)} fusion(bf16[1024,1024]{1,0:T(8,128)(2,1)} %bitcast.14, bf16[768,1024]{1,0:T(8,128)(2,1)} %bitcast.117), kind=kOutput, calls=%fused_computation.26 | convolution fusion | flops 1611399168 | bytes 5242880 | tf_op jit(solution)/shard_map/dot_general | solution.py:16
  431.7 18.7 %all-to-all-done.11 = bf16[8,144,1024]{2,1,0:T(8,128)(2,1)} async-done(((bf16[8,144,1024]{2,1,0:T(8,128)(2,1)}), bf16[8,144,1024]{2,1,0:T(8,128)(2,1)}, u32[]{:S(2)}, u32[]{:S(2)}) %all-to-all-start.11) | async-done | bytes 2359328 | tf_op jit(solution)/shard_map/all_to_all | solution.py:27
  453.4 6.1 %all-to-all-start.12 = ((bf16[4,48,1024]{2,1,0:T(8,128)(2,1)}), bf16[4,48,1024]{2,1,0:T(8,128)(2,1)S(1)}, u32[]{:S(2)}, u32[]{:S(2)}) async-start(bf16[4,48,1024]{2,1,0:T(8,128)(2,1)} %pad_maximum_fusion.4), calls=%async_computation.14 | async-start | bytes 786432 | tf_op jit(solution)/shard_map/all_to_all | solution.py:27
  463.5 32.0 %reduce-scatter.5.cloned.1.call-done = bf16[128,384]{1,0:T(8,128)(2,1)} async-done(((bf16[1024,384]{1,0:T(8,128)(2,1)}), bf16[128,384]{1,0:T(8,128)(2,1)}) %reduce-scatter.5.cloned.1.call-update) | async-done | bytes 98320 | tf_op jit(solution)/shard_map/reduce_scatter | solution.py:149
  (166 shorter events, 65.7 us)
Async XLA Ops:
  7.2 68.6 %copy-start = (bf16[128,1024]{1,0:T(8,128)(2,1)S(1)}, bf16[128,1024]{1,0:T(8,128)(2,1)}, u32[]{:S(2)}) copy-start(bf16[128,1024]{1,0:T(8,128)(2,1)} %param.19) | copy-start | bytes 786436
  29.1 42.7 %copy-start.24 = (f32[1024]{0:T(1024)S(1)}, f32[1024]{0:T(1024)}, u32[]{:S(2)}) copy-start(f32[1024]{0:T(1024)} %param.16) | copy-start | bytes 12292
  29.1 42.9 %copy-start.13 = (bf16[1024,128]{1,0:T(8,128)(2,1)S(1)}, bf16[1024,128]{1,0:T(8,128)(2,1)}, u32[]{:S(2)}) copy-start(bf16[1024,128]{1,0:T(8,128)(2,1)} %param.18) | copy-start | bytes 786436
  29.1 42.9 %copy-start.14 = (bf16[1024,128]{1,0:T(8,128)(2,1)S(1)}, bf16[1024,128]{1,0:T(8,128)(2,1)}, u32[]{:S(2)}) copy-start(bf16[1024,128]{1,0:T(8,128)(2,1)} %param.17) | copy-start | bytes 786436
  29.1 43.0 %all-to-all-start.1 = ((bf16[8,128,1024]{2,1,0:T(8,128)(2,1)}), bf16[8,128,1024]{2,1,0:T(8,128)(2,1)S(1)}, u32[]{:S(2)}, u32[]{:S(2)}) async-start(bf16[8,128,1024]{2,1,0:T(8,128)(2,1)} %broadcast_in_dim.30), calls=%async_computation.1 | async-start | bytes 4194304 | tf_op jit(solution)/shard_map/all_to_all | solution.py:21
  34.1 199.8 %all-gather.2.cloned.1.call-start = ((), (), s32[]{:S(2)}) async-start(), calls=%async_computation.15 | async-start | bytes 5898240 | tf_op jit(solution)/shard_map/all_gather | solution.py:67
  128.4 20.0 %copy-start.20 = (f32[1024]{0:T(1024)S(1)}, f32[1024]{0:T(1024)}, u32[]{:S(2)}) copy-start(f32[1024]{0:T(1024)} %param.20) | copy-start | bytes 12292
  131.1 16.6 %all-to-all-start.3 = ((bf16[4,32,1024]{2,1,0:T(8,128)(2,1)}), bf16[4,32,1024]{2,1,0:T(8,128)(2,1)S(1)}, u32[]{:S(2)}, u32[]{:S(2)}) async-start(bf16[4,32,1024]{2,1,0:T(8,128)(2,1)} %bitcast.12), calls=%async_computation.3 | async-start | bytes 524288 | tf_op jit(solution)/shard_map/all_to_all | solution.py:27
  166.9 80.4 %all-to-all-start.5 = ((bf16[8,128,1024]{2,1,0:T(8,128)(2,1)}), bf16[8,128,1024]{2,1,0:T(8,128)(2,1)}, u32[]{:S(2)}, u32[]{:S(2)}) async-start(bf16[8,128,1024]{2,1,0:T(8,128)(2,1)} %broadcast_in_dim.33), calls=%async_computation.5 | async-start | bytes 4194304 | tf_op jit(solution)/shard_map/all_to_all | solution.py:21
  174.2 6.7 %copy-start.23 = (s32[1024]{0:T(1024)S(1)}, s32[1024]{0:T(1024)}, u32[]{:S(2)}) copy-start(s32[1024]{0:T(1024)} %param.23) | copy-start | bytes 12292
  255.8 29.1 %copy-start.2 = (f32[256,1024]{1,0:T(8,128)S(1)}, f32[256,1024]{1,0:T(8,128)}, u32[]{:S(2)}) copy-start(f32[256,1024]{1,0:T(8,128)} %get-tuple-element.78) | copy-start | bytes 3145732
  346.4 19.9 %copy-start.21 = (f32[1024]{0:T(1024)S(1)}, f32[1024]{0:T(1024)}, u32[]{:S(2)}) copy-start(f32[1024]{0:T(1024)} %param.20) | copy-start | bytes 12292
  346.4 20.0 %copy-start.26 = (f32[32]{0:T(128)S(1)}, f32[32]{0:T(128)}, u32[]{:S(2)}) copy-start(f32[32]{0:T(128)} %copy-done.25) | copy-start | bytes 388
  346.4 20.0 %copy-start.27 = (f32[32]{0:T(128)S(1)}, f32[32]{0:T(128)}, u32[]{:S(2)}) copy-start(f32[32]{0:T(128)} %get-tuple-element.98) | copy-start | bytes 388
  380.6 29.0 %all-to-all-start.10 = ((bf16[8,128,1024]{1,2,0:T(8,128)(2,1)}), bf16[8,128,1024]{1,2,0:T(8,128)(2,1)}, u32[]{:S(2)}, u32[]{:S(2)}) async-start(bf16[8,128,1024]{1,2,0:T(8,128)(2,1)} %broadcast_in_dim.38), calls=%async_computation.11 | async-start | bytes 4194304 | tf_op jit(solution)/shard_map/all_to_all | solution.py:21
  385.2 28.4 %copy-start.5 = (f32[256,1024]{1,0:T(8,128)S(1)}, f32[256,1024]{1,0:T(8,128)}, u32[]{:S(2)}) copy-start(f32[256,1024]{1,0:T(8,128)} %copy-done.4) | copy-start | bytes 3145732
  418.7 31.6 %all-to-all-start.11 = ((bf16[8,144,1024]{2,1,0:T(8,128)(2,1)}), bf16[8,144,1024]{2,1,0:T(8,128)(2,1)}, u32[]{:S(2)}, u32[]{:S(2)}) async-start(bf16[8,144,1024]{2,1,0:T(8,128)(2,1)} %pad_maximum_fusion), calls=%async_computation.13 | async-start | bytes 4718592 | tf_op jit(solution)/shard_map/all_to_all | solution.py:27
  423.1 5.2 %copy-start.19 = (f32[1024]{0:T(1024)S(1)}, f32[1024]{0:T(1024)}, u32[]{:S(2)}) copy-start(f32[1024]{0:T(1024)} %copy-done.18) | copy-start | bytes 12292
  423.1 5.2 %copy-start.29 = (bf16[128,1024]{1,0:T(8,128)(2,1)S(1)}, bf16[128,1024]{1,0:T(8,128)(2,1)}, u32[]{:S(2)}) copy-start(bf16[128,1024]{1,0:T(8,128)(2,1)} %copy-done.28) | copy-start | bytes 786436
  423.1 5.2 %copy-start.31 = (bf16[128,1024]{1,0:T(8,128)(2,1)S(1)}, bf16[128,1024]{1,0:T(8,128)(2,1)}, u32[]{:S(2)}) copy-start(bf16[128,1024]{1,0:T(8,128)(2,1)} %copy-done.30) | copy-start | bytes 786436
  423.1 37.2 %reduce-scatter.3.cloned.1.call-start = ((), (), s32[]{:S(2)}) async-start(), calls=%async_computation.16 | async-start | bytes 1769472 | tf_op jit(solution)/shard_map/reduce_scatter | solution.py:132
  428.3 67.2 %reduce-scatter.5.cloned.1.call-start = ((), (), s32[]{:S(2)}) async-start(), calls=%async_computation.17 | async-start | bytes 884736 | tf_op jit(solution)/shard_map/reduce_scatter | solution.py:149
  453.4 45.2 %copy-start.12 = (bf16[1024,32]{0,1:T(8,128)(2,1)S(1)}, bf16[1024,32]{0,1:T(8,128)(2,1)}, u32[]{:S(2)}) copy-start(bf16[1024,32]{0,1:T(8,128)(2,1)} %param.15) | copy-start | bytes 196612
  453.4 45.1 %all-to-all-start.12 = ((bf16[4,48,1024]{2,1,0:T(8,128)(2,1)}), bf16[4,48,1024]{2,1,0:T(8,128)(2,1)S(1)}, u32[]{:S(2)}, u32[]{:S(2)}) async-start(bf16[4,48,1024]{2,1,0:T(8,128)(2,1)} %pad_maximum_fusion.4), calls=%async_computation.14 | async-start | bytes 786432 | tf_op jit(solution)/shard_map/all_to_all | solution.py:27
  (17 other events, 35.1 us)
Sparse Core Ops, SparseCore 0:
  71.9 161.9 all-gather.1
  428.4 31.6 reduce-scatter.2
  462.7 32.7 reduce-scatter.4

commit v2 on v1

--- a/solution.py
+++ b/solution.py
@@ -63,8 +63,7 @@
     student_flat = student_head.reshape(width_s, level_count * code_count)
     level_mask = (jnp.arange(level_count, dtype=jnp.int32)[:, None] == levels[None, :]).astype(F32)
 
-    teacher_t = lax.all_gather(teacher_hidden.T, OUTER, axis=0, tiled=True)
-    teacher_t = lax.all_gather(teacher_t, INNER, axis=0, tiled=True)
+    teacher_t = spread(spread(teacher_hidden.T, OUTER, outer), INNER, inner)
 
     own_cols = student_hidden.T
     student_t = spread(spread(own_cols, OUTER, outer), INNER, inner)
@@ -88,7 +87,23 @@
     mixed_rows = from_gathered(student_own).T + down_own
     scale_out = lax.rsqrt(jnp.mean(mixed_rows * mixed_rows, axis=1) + NORM_EPS)
     normed_own = (mixed_rows * scale_out[:, None] * final_gain).astype(BF16)
-    normed_out = spread(spread(normed_own, OUTER, outer), INNER, inner)
+
+    centre_part = jnp.mean(student_head.astype(F32), axis=2).T
+    centre_part = jnp.pad(centre_part, ((0, 16 - level_count), (0, 0)))
+    sent = spread(jnp.concatenate([normed_own, centre_part.astype(BF16)]), OUTER, outer)
+    sent = sent.reshape(outer, -1, width_s)
+    centre_part = jnp.mean(sent[:, own_rows:].astype(F32), axis=0)
+    sent = jnp.concatenate(
+        [sent[:, :own_rows].reshape(-1, width_s), centre_part.astype(BF16)], axis=0
+    )
+    sent = spread(sent, INNER, inner).reshape(inner, -1, width_s)
+    normed_out = sent[:, : outer * own_rows].reshape(row_count, width_s)
+    centre = jnp.mean(sent[:, outer * own_rows :].astype(F32), axis=0)[:level_count]
+    student_centred = (
+        (student_head.astype(F32) - centre.T[:, :, None])
+        .astype(BF16)
+        .reshape(width_s, level_count * code_count)
+    )
 
     teacher_wide = from_gathered(teacher_t).astype(F32)
     teacher_scale = lax.rsqrt(jnp.mean(teacher_wide * teacher_wide, axis=0) + NORM_EPS)
@@ -126,10 +141,10 @@
         .reshape(level_count * code_count, row_count)
     )
 
-    code_part = dot(grad_full, student_flat, 0, 1)
-    back_out = collect(collect(code_part, INNER, inner), OUTER, outer)
+    code_part = dot(grad_full, student_centred, 0, 1).astype(BF16)
+    back_out = collect(collect(code_part, INNER, inner).astype(BF16), OUTER, outer)
     head_term = dot(normed_out, grad_full, 0, 1).astype(BF16)
-    head_share = lax.psum_scatter(head_term, ROWS, scatter_dimension=0, tiled=True).astype(F32)
+    head_share = collect(head_term, ROWS, dp)
     gained = final_gain * back_out
     back_mixed = (
         scale_out[:, None] * gained
@@ -146,9 +161,7 @@
     )
     both_term = from_gathered(dot(normed_in, back_both, 1, 1).astype(BF16))
     down_term = dot(back_mixed_b, hidden, 0, 1).astype(BF16)
-    grad_share = lax.psum_scatter(
-        jnp.concatenate([both_term, down_term], axis=1), ROWS, scatter_dimension=0, tiled=True
-    ).astype(F32)
+    grad_share = collect(jnp.concatenate([both_term, down_term], axis=1), ROWS, dp)
     gate_share = grad_share[:, :units]
     up_share = grad_share[:, units : 2 * units]
     down_share = grad_share[:, 2 * units :].T

time: 511 us -> 457 us (0.89)
  blocking collectives: 233 us -> 87.5 us
  waiting for transfers between devices: 140 us -> 210 us
  starting transfers between devices: 28.7 us -> 53.3 us
  between operations: 14.4 us -> 1.32 us
  other arithmetic: 31.4 us -> 41.1 us
  local copies, waits for them, and re-layouts: 34.4 us -> 41.1 us
    all_to_all x3 -> x6, waiting for transfers between devices: 24.3 us -> 124 us  [spread(): got = lax.all_to_all(copies, axes, 0, 0, tiled=True)]
    all_to_all x3 -> x2, blocking collectives: 123 us -> 41.5 us  [collect(): got = lax.all_to_all(parts, axes, 0, 0, tiled=True)]
    all_to_all x3 -> x6, waiting for transfers between devices: 30.4 us -> 85.5 us  [collect(): got = lax.all_to_all(parts, axes, 0, 0, tiled=True)]
    all_gather x1 -> x0, waiting for transfers between devices: 53 us -> none  [body(): teacher_t = lax.all_gather(teacher_t, INNER, axis=0, tiled=True)]
    all_gather x1 -> x0, blocking collectives: 37.6 us -> none  [body(): teacher_t = lax.all_gather(teacher_hidden.T, OUTER, axis=0, tiled=True)]
    reduce_scatter x2 -> x0, waiting for transfers between devices: 32 us -> none  [the longest x1 32 us: body(): lax.psum_scatter(jnp.concatenate([both_term, down_term], axis=1), ROWS, s...]
    all_to_all x4 -> x3, blocking collectives: 72.3 us -> 46 us  [spread(): got = lax.all_to_all(copies, axes, 0, 0, tiled=True)]
    all_to_all x3 -> x6, starting transfers between devices: 14.1 us -> 27.9 us  [spread(): got = lax.all_to_all(copies, axes, 0, 0, tiled=True)]
  transfers between devices with their start and end apart: 9 -> 12, of which waited for: 5 -> 12; matrix products, arithmetic and copies ran while one was open for 9% -> 13% of each run, Pallas kernels for 0% -> 0%
where the time goes in v2:
time: 457 us; the launch traced here: 455 us
  waiting for transfers between devices  210 us (46%)
  blocking collectives  87.5 us (19%)
  starting transfers between devices  53.3 us (12%)
  local copies, waits for them, and re-layouts  41.1 us (9%)
  other arithmetic  41.1 us (9%)
  matrix products  20.8 us (5%)
    all_to_all x6, waiting for transfers between devices, spread(): got = lax.all_to_all(copies, axes, 0, 0, tiled=True)  124 us
    all_to_all x6, waiting for transfers between devices, collect(): got = lax.all_to_all(parts, axes, 0, 0, tiled=True)  85.5 us
    all_to_all x3, blocking collectives, spread(): got = lax.all_to_all(copies, axes, 0, 0, tiled=True)  46 us
    all_to_all x2, blocking collectives, collect(): got = lax.all_to_all(parts, axes, 0, 0, tiled=True)  41.5 us
    all_to_all x6, starting transfers between devices, spread(): got = lax.all_to_all(copies, axes, 0, 0, tiled=True)  27.9 us
    all_to_all x6, starting transfers between devices, collect(): got = lax.all_to_all(parts, axes, 0, 0, tiled=True)  25.4 us
    dot_general x10, matrix products, dot(): lax.dot_general(a, b, (((da,), (db,)), ((), ())), preferred_element_type=...  20.8 us
    unnamed x81, local copies, waits for them, and re-layouts  16.9 us
  transfers between devices with their start and end apart: 12, of which 12 were waited for; matrix products, arithmetic and copies ran while one was open for 13% of the time, Pallas kernels for 0%

profile of v2, /device:TPU:2, one launch (start us, length us, event | category | flops | bytes accessed | tf_op | source)
XLA Modules:
  0.0 454.8 jit_solution(9081775593808643466)
XLA Ops:
  1.6 19.3 %all_to_all.85 = bf16[4,32,1024]{2,1,0:T(8,128)(2,1)S(1)} all-to-all(bf16[4,32,1024]{2,1,0:T(8,128)(2,1)S(1)} %broadcast_in_dim.31), channel_id=1, replica_groups=mesh['zh'=4,'x'=4,'core'=2,'y'=4,'zl'=2] {'zh'}, dimensions={0} | all-to-all | bytes 524288 | tf_op jit(solution)/shard_map/all_to_all | solution.py:21
  22.5 5.0 %all-to-all-start.1 = ((bf16[8,128,1024]{2,1,0:T(8,128)(2,1)}), bf16[8,128,1024]{2,1,0:T(8,128)(2,1)S(1)}, u32[]{:S(2)}, u32[]{:S(2)}) async-start(bf16[8,128,1024]{2,1,0:T(8,128)(2,1)} %broadcast_in_dim.33), calls=%async_computation.1 | async-start | bytes 4194304 | tf_op jit(solution)/shard_map/all_to_all | solution.py:21
  27.8 24.8 %all-to-all-done.1 = bf16[8,128,1024]{2,1,0:T(8,128)(2,1)S(1)} async-done(((bf16[8,128,1024]{2,1,0:T(8,128)(2,1)}), bf16[8,128,1024]{2,1,0:T(8,128)(2,1)S(1)}, u32[]{:S(2)}, u32[]{:S(2)}) %all-to-all-start.1) | async-done | bytes 2097184 | tf_op jit(solution)/shard_map/all_to_all | solution.py:21
  62.7 25.2 %all-to-all-done.2 = bf16[8,128,1024]{2,1,0:T(8,128)(2,1)} async-done(((bf16[8,128,1024]{2,1,0:T(8,128)(2,1)}), bf16[8,128,1024]{2,1,0:T(8,128)(2,1)}, u32[]{:S(2)}, u32[]{:S(2)}) %all-to-all-start.2) | async-done | bytes 2097184 | tf_op jit(solution)/shard_map/all_to_all | solution.py:27
  96.0 7.6 %all-to-all-done.3 = bf16[4,32,1024]{2,1,0:T(8,128)(2,1)S(1)} async-done(((bf16[4,32,1024]{2,1,0:T(8,128)(2,1)}), bf16[4,32,1024]{2,1,0:T(8,128)(2,1)S(1)}, u32[]{:S(2)}, u32[]{:S(2)}) %all-to-all-start.3) | async-done | bytes 262176 | tf_op jit(solution)/shard_map/all_to_all | solution.py:27
  114.3 8.2 %all-to-all-done.6 = bf16[4,80,1024]{2,1,0:T(8,128)(2,1)S(1)} async-done(((bf16[4,80,1024]{2,1,0:T(8,128)(2,1)}), bf16[4,80,1024]{2,1,0:T(8,128)(2,1)S(1)}, u32[]{:S(2)}, u32[]{:S(2)}) %all-to-all-start.6) | async-done | bytes 655392 | tf_op jit(solution)/shard_map/all_to_all | solution.py:21
  122.6 14.6 %all_to_all.86 = bf16[4,48,1024]{2,1,0:T(8,128)(2,1)S(1)} all-to-all(bf16[4,48,1024]{2,1,0:T(8,128)(2,1)S(1)} %broadcast_in_dim.34), channel_id=1, replica_groups=mesh['zh'=4,'x'=4,'core'=2,'y'=4,'zl'=2] {'zh'}, dimensions={0} | all-to-all | bytes 786432 | tf_op jit(solution)/shard_map/all_to_all | solution.py:21
  140.2 5.6 %all-to-all-start.7 = ((bf16[8,320,1024]{2,1,0:T(8,128)(2,1)}), bf16[8,320,1024]{2,1,0:T(8,128)(2,1)}, u32[]{:S(2)}, u32[]{:S(2)}) async-start(bf16[8,320,1024]{2,1,0:T(8,128)(2,1)} %broadcast_in_dim.39), calls=%async_computation.7 | async-start | bytes 10485760 | tf_op jit(solution)/shard_map/all_to_all | solution.py:21
  145.8 55.4 %all-to-all-done.7 = bf16[8,320,1024]{2,1,0:T(8,128)(2,1)} async-done(((bf16[8,320,1024]{2,1,0:T(8,128)(2,1)}), bf16[8,320,1024]{2,1,0:T(8,128)(2,1)}, u32[]{:S(2)}, u32[]{:S(2)}) %all-to-all-start.7) | async-done | bytes 5242912 | tf_op jit(solution)/shard_map/all_to_all | solution.py:21
  203.0 4.6 %all-to-all-start.5 = ((bf16[8,144,1024]{2,1,0:T(8,128)(2,1)}), bf16[8,144,1024]{2,1,0:T(8,128)(2,1)}, u32[]{:S(2)}, u32[]{:S(2)}) async-start(bf16[8,144,1024]{2,1,0:T(8,128)(2,1)} %broadcast_in_dim.35), calls=%async_computation.5 | async-start | bytes 4718592 | tf_op jit(solution)/shard_map/all_to_all | solution.py:21
  210.3 6.2 %copy.145 = bf16[2560,3,256]{0,2,1:T(8,128)(2,1)} copy(bf16[2560,3,256]{2,0,1:T(8,128)(2,1)} %param.14) | data formatting | bytes 7864320 | tf_op args[2]
  226.5 5.9 %fusion.44 = f32[1024,768]{0,1:T(8,128)} fusion(bf16[2560,768]{0,1:T(8,128)(2,1)S(1)} %bitcast.118, bf16[2560,1024]{1,0:T(8,128)(2,1)S(1)} %bitcast.117), kind=kOutput, calls=%fused_computation.122 | convolution fusion | flops 4026531840 | bytes 12320768 | tf_op jit(solution)/shard_map/dot_general | solution.py:16
  248.3 4.8 %all-to-all-start.8 = ((f32[32,4,1024]{2,1,0:T(4,128)}), f32[32,4,1024]{2,1,0:T(4,128)}, u32[]{:S(2)}, u32[]{:S(2)}) async-start(f32[32,4,1024]{2,1,0:T(4,128)} %broadcast_in_dim.41), calls=%async_computation.8 | async-start | bytes 1048576 | tf_op jit(solution)/shard_map/all_to_all | solution.py:21
  254.8 14.4 %all-to-all-done.8 = f32[32,4,1024]{2,1,0:T(4,128)} async-done(((f32[32,4,1024]{2,1,0:T(4,128)}), f32[32,4,1024]{2,1,0:T(4,128)}, u32[]{:S(2)}, u32[]{:S(2)}) %all-to-all-start.8) | async-done | bytes 524320 | tf_op jit(solution)/shard_map/all_to_all | solution.py:21
  276.7 29.5 %all_to_all.87 = bf16[8,128,1024]{2,1,0:T(8,128)(2,1)} all-to-all(bf16[8,128,1024]{2,1,0:T(8,128)(2,1)S(1)} %bitcast.129), channel_id=1, replica_groups=mesh['zh'=4,'x'=4,'core'=2,'y'=4,'zl'=2] {'y','zl'}, dimensions={0} | all-to-all | bytes 4194304 | tf_op jit(solution)/shard_map/all_to_all | solution.py:27
  308.2 12.0 %all_to_all.88 = bf16[4,32,1024]{2,1,0:T(8,128)(2,1)S(1)} all-to-all(bf16[4,32,1024]{2,1,0:T(8,128)(2,1)S(1)} %bitcast.139), channel_id=1, replica_groups=mesh['zh'=4,'x'=4,'core'=2,'y'=4,'zl'=2] {'zh'}, dimensions={0} | all-to-all | bytes 524288 | tf_op jit(solution)/shard_map/all_to_all | solution.py:27
  320.5 12.1 %all_to_all.89 = bf16[4,32,1024]{2,1,0:T(8,128)(2,1)S(1)} all-to-all(bf16[4,32,1024]{2,1,0:T(8,128)(2,1)S(1)} %broadcast_in_dim.42), channel_id=1, replica_groups=mesh['zh'=4,'x'=4,'core'=2,'y'=4,'zl'=2] {'zh'}, dimensions={0} | all-to-all | bytes 524288 | tf_op jit(solution)/shard_map/all_to_all | solution.py:21
  343.5 17.9 %all-to-all-done.13 = bf16[8,128,1024]{1,2,0:T(8,128)(2,1)} async-done(((bf16[8,128,1024]{1,2,0:T(8,128)(2,1)}), bf16[8,128,1024]{1,2,0:T(8,128)(2,1)}, u32[]{:S(2)}, u32[]{:S(2)}) %all-to-all-start.13) | async-done | bytes 2097184 | tf_op jit(solution)/shard_map/all_to_all | solution.py:21
  361.5 4.9 %all-to-all-start.9 = ((bf16[8,128,768]{2,1,0:T(8,128)(2,1)}), bf16[8,128,768]{2,1,0:T(8,128)(2,1)}, u32[]{:S(2)}, u32[]{:S(2)}) async-start(bf16[8,128,768]{2,1,0:T(8,128)(2,1)} %bitcast.132), calls=%async_computation.9 | async-start | bytes 3145728 | tf_op jit(solution)/shard_map/all_to_all | solution.py:27
  375.7 10.8 %all-to-all-done.9 = bf16[8,128,768]{2,1,0:T(8,128)(2,1)} async-done(((bf16[8,128,768]{2,1,0:T(8,128)(2,1)}), bf16[8,128,768]{2,1,0:T(8,128)(2,1)}, u32[]{:S(2)}, u32[]{:S(2)}) %all-to-all-start.9) | async-done | bytes 1572896 | tf_op jit(solution)/shard_map/all_to_all | solution.py:27
  395.1 25.7 %all-to-all-done.15 = bf16[8,144,1024]{2,1,0:T(8,128)(2,1)} async-done(((bf16[8,144,1024]{2,1,0:T(8,128)(2,1)}), bf16[8,144,1024]{2,1,0:T(8,128)(2,1)}, u32[]{:S(2)}, u32[]{:S(2)}) %all-to-all-start.15) | async-done | bytes 2359328 | tf_op jit(solution)/shard_map/all_to_all | solution.py:27
  420.8 4.9 %all-to-all-start.14 = ((bf16[8,128,384]{2,1,0:T(8,128)(2,1)}), bf16[8,128,384]{2,1,0:T(8,128)(2,1)S(1)}, u32[]{:S(2)}, u32[]{:S(2)}) async-start(bf16[8,128,384]{2,1,0:T(8,128)(2,1)} %pad_maximum_fusion.1), calls=%async_computation.14 | async-start | bytes 1572864 | tf_op jit(solution)/shard_map/all_to_all | solution.py:27
  428.8 8.6 %all-to-all-done.14 = bf16[8,128,384]{2,1,0:T(8,128)(2,1)S(1)} async-done(((bf16[8,128,384]{2,1,0:T(8,128)(2,1)}), bf16[8,128,384]{2,1,0:T(8,128)(2,1)S(1)}, u32[]{:S(2)}, u32[]{:S(2)}) %all-to-all-start.14) | async-done | bytes 786464 | tf_op jit(solution)/shard_map/all_to_all | solution.py:27
  446.4 7.5 %all-to-all-done.16 = bf16[4,48,1024]{2,1,0:T(8,128)(2,1)S(1)} async-done(((bf16[4,48,1024]{2,1,0:T(8,128)(2,1)}), bf16[4,48,1024]{2,1,0:T(8,128)(2,1)S(1)}, u32[]{:S(2)}, u32[]{:S(2)}) %all-to-all-start.16) | async-done | bytes 393248 | tf_op jit(solution)/shard_map/all_to_all | solution.py:27
  (188 shorter events, 117.8 us)
Async XLA Ops:
  0.6 55.7 %copy-start = (bf16[128,1024]{1,0:T(8,128)(2,1)S(1)}, bf16[128,1024]{1,0:T(8,128)(2,1)}, u32[]{:S(2)}) copy-start(bf16[128,1024]{1,0:T(8,128)(2,1)} %param.19) | copy-start | bytes 786436
  22.5 30.1 %all-to-all-start.1 = ((bf16[8,128,1024]{2,1,0:T(8,128)(2,1)}), bf16[8,128,1024]{2,1,0:T(8,128)(2,1)S(1)}, u32[]{:S(2)}, u32[]{:S(2)}) async-start(bf16[8,128,1024]{2,1,0:T(8,128)(2,1)} %broadcast_in_dim.33), calls=%async_computation.1 | async-start | bytes 4194304 | tf_op jit(solution)/shard_map/all_to_all | solution.py:21
  27.6 26.1 %copy-start.21 = (f32[8,4,32]{2,1,0:T(4,128)}, f32[8,4,32]{2,1,0:T(4,128)S(1)}, u32[]{:S(2)}) copy-start(f32[8,4,32]{2,1,0:T(4,128)S(1)} %copy.141) | copy-start | bytes 12292
  27.8 25.9 %copy-start.11 = (bf16[8,4,32,256]{3,2,1,0:T(8,128)(2,1)}, bf16[8,4,32,256]{3,2,1,0:T(8,128)(2,1)S(1)}, u32[]{:S(2)}) copy-start(bf16[8,4,32,256]{3,2,1,0:T(8,128)(2,1)S(1)} %copy.140) | copy-start | bytes 1572868
  58.3 29.6 %all-to-all-start.2 = ((bf16[8,128,1024]{2,1,0:T(8,128)(2,1)}), bf16[8,128,1024]{2,1,0:T(8,128)(2,1)}, u32[]{:S(2)}, u32[]{:S(2)}) async-start(bf16[8,128,1024]{2,1,0:T(8,128)(2,1)} %bitcast.115), calls=%async_computation.2 | async-start | bytes 4194304 | tf_op jit(solution)/shard_map/all_to_all | solution.py:27
  62.7 40.9 %copy-start.20 = (bf16[1024,80]{0,1:T(8,128)(2,1)S(1)}, bf16[1024,80]{0,1:T(8,128)(2,1)}, u32[]{:S(2)}) copy-start(bf16[1024,80]{0,1:T(8,128)(2,1)} %param.12) | copy-start | bytes 491524
  90.6 13.0 %all-to-all-start.3 = ((bf16[4,32,1024]{2,1,0:T(8,128)(2,1)}), bf16[4,32,1024]{2,1,0:T(8,128)(2,1)S(1)}, u32[]{:S(2)}, u32[]{:S(2)}) async-start(bf16[4,32,1024]{2,1,0:T(8,128)(2,1)} %bitcast.12), calls=%async_computation.3 | async-start | bytes 524288 | tf_op jit(solution)/shard_map/all_to_all | solution.py:27
  104.5 18.0 %all-to-all-start.6 = ((bf16[4,80,1024]{2,1,0:T(8,128)(2,1)}), bf16[4,80,1024]{2,1,0:T(8,128)(2,1)S(1)}, u32[]{:S(2)}, u32[]{:S(2)}) async-start(bf16[4,80,1024]{2,1,0:T(8,128)(2,1)} %broadcast_in_dim.36), calls=%async_computation.6 | async-start | bytes 1310720 | tf_op jit(solution)/shard_map/all_to_all | solution.py:21
  140.2 61.1 %all-to-all-start.7 = ((bf16[8,320,1024]{2,1,0:T(8,128)(2,1)}), bf16[8,320,1024]{2,1,0:T(8,128)(2,1)}, u32[]{:S(2)}, u32[]{:S(2)}) async-start(bf16[8,320,1024]{2,1,0:T(8,128)(2,1)} %broadcast_in_dim.39), calls=%async_computation.7 | async-start | bytes 10485760 | tf_op jit(solution)/shard_map/all_to_all | solution.py:21
  203.0 32.8 %all-to-all-start.5 = ((bf16[8,144,1024]{2,1,0:T(8,128)(2,1)}), bf16[8,144,1024]{2,1,0:T(8,128)(2,1)}, u32[]{:S(2)}, u32[]{:S(2)}) async-start(bf16[8,144,1024]{2,1,0:T(8,128)(2,1)} %broadcast_in_dim.35), calls=%async_computation.5 | async-start | bytes 4718592 | tf_op jit(solution)/shard_map/all_to_all | solution.py:21
  248.3 20.9 %all-to-all-start.8 = ((f32[32,4,1024]{2,1,0:T(4,128)}), f32[32,4,1024]{2,1,0:T(4,128)}, u32[]{:S(2)}, u32[]{:S(2)}) async-start(f32[32,4,1024]{2,1,0:T(4,128)} %broadcast_in_dim.41), calls=%async_computation.8 | async-start | bytes 1048576 | tf_op jit(solution)/shard_map/all_to_all | solution.py:21
  306.2 14.0 %copy-start.26 = (f32[1024]{0:T(1024)S(1)}, f32[1024]{0:T(1024)}, u32[]{:S(2)}) copy-start(f32[1024]{0:T(1024)} %param.20) | copy-start | bytes 12292
  306.2 14.2 %copy-start.32 = (f32[32]{0:T(128)S(1)}, f32[32]{0:T(128)}, u32[]{:S(2)}) copy-start(f32[32]{0:T(128)} %copy-done.31) | copy-start | bytes 388
  306.2 14.2 %copy-start.33 = (f32[32]{0:T(128)S(1)}, f32[32]{0:T(128)}, u32[]{:S(2)}) copy-start(f32[32]{0:T(128)} %get-tuple-element.99) | copy-start | bytes 388
  334.4 27.0 %all-to-all-start.13 = ((bf16[8,128,1024]{1,2,0:T(8,128)(2,1)}), bf16[8,128,1024]{1,2,0:T(8,128)(2,1)}, u32[]{:S(2)}, u32[]{:S(2)}) async-start(bf16[8,128,1024]{1,2,0:T(8,128)(2,1)} %broadcast_in_dim.44), calls=%async_computation.13 | async-start | bytes 4194304 | tf_op jit(solution)/shard_map/all_to_all | solution.py:21
  343.5 22.8 %copy-start.22 = (f32[8,4,32]{2,1,0:T(4,128)S(1)}, f32[8,4,32]{2,1,0:T(4,128)}, u32[]{:S(2)}) copy-start(f32[8,4,32]{2,1,0:T(4,128)} %copy-done.21) | copy-start | bytes 12292
  361.5 25.1 %all-to-all-start.9 = ((bf16[8,128,768]{2,1,0:T(8,128)(2,1)}), bf16[8,128,768]{2,1,0:T(8,128)(2,1)}, u32[]{:S(2)}, u32[]{:S(2)}) async-start(bf16[8,128,768]{2,1,0:T(8,128)(2,1)} %bitcast.132), calls=%async_computation.9 | async-start | bytes 3145728 | tf_op jit(solution)/shard_map/all_to_all | solution.py:27
  375.7 16.0 %copy-start.24 = (f32[1024]{0:T(1024)S(1)}, f32[1024]{0:T(1024)}, u32[]{:S(2)}) copy-start(f32[1024]{0:T(1024)} %copy-done.23) | copy-start | bytes 12292
  375.7 16.0 %copy-start.35 = (bf16[128,1024]{1,0:T(8,128)(2,1)S(1)}, bf16[128,1024]{1,0:T(8,128)(2,1)}, u32[]{:S(2)}) copy-start(bf16[128,1024]{1,0:T(8,128)(2,1)} %copy-done.34) | copy-start | bytes 786436
  375.7 16.0 %copy-start.37 = (bf16[128,1024]{1,0:T(8,128)(2,1)S(1)}, bf16[128,1024]{1,0:T(8,128)(2,1)}, u32[]{:S(2)}) copy-start(bf16[128,1024]{1,0:T(8,128)(2,1)} %copy-done.36) | copy-start | bytes 786436
  386.6 34.3 %all-to-all-start.15 = ((bf16[8,144,1024]{2,1,0:T(8,128)(2,1)}), bf16[8,144,1024]{2,1,0:T(8,128)(2,1)}, u32[]{:S(2)}, u32[]{:S(2)}) async-start(bf16[8,144,1024]{2,1,0:T(8,128)(2,1)} %pad_maximum_fusion), calls=%async_computation.15 | async-start | bytes 4718592 | tf_op jit(solution)/shard_map/all_to_all | solution.py:27
  420.8 16.6 %all-to-all-start.14 = ((bf16[8,128,384]{2,1,0:T(8,128)(2,1)}), bf16[8,128,384]{2,1,0:T(8,128)(2,1)S(1)}, u32[]{:S(2)}, u32[]{:S(2)}) async-start(bf16[8,128,384]{2,1,0:T(8,128)(2,1)} %pad_maximum_fusion.1), calls=%async_computation.14 | async-start | bytes 1572864 | tf_op jit(solution)/shard_map/all_to_all | solution.py:27
  437.5 16.4 %all-to-all-start.16 = ((bf16[4,48,1024]{2,1,0:T(8,128)(2,1)}), bf16[4,48,1024]{2,1,0:T(8,128)(2,1)S(1)}, u32[]{:S(2)}, u32[]{:S(2)}) async-start(bf16[4,48,1024]{2,1,0:T(8,128)(2,1)} %pad_maximum_fusion.4), calls=%async_computation.16 | async-start | bytes 786432 | tf_op jit(solution)/shard_map/all_to_all | solution.py:27
  442.6 11.4 %copy-start.17 = (bf16[1024,32]{0,1:T(8,128)(2,1)S(1)}, bf16[1024,32]{0,1:T(8,128)(2,1)}, u32[]{:S(2)}) copy-start(bf16[1024,32]{0,1:T(8,128)(2,1)} %param.15) | copy-start | bytes 196612
  (26 other events, 78.9 us)

commit v3 on v2

--- a/solution.py
+++ b/solution.py
@@ -4,8 +4,8 @@
 from jax.sharding import Mesh, PartitionSpec as P
 
 NORM_EPS = 1e-06
-OUTER = "zh"
-INNER = ("y", "zl")
+OUTER = ("zh", "zl")
+INNER = "y"
 GROUP = ("zh", "y", "zl")
 ROWS = ("x", "core")
 F32 = jnp.float32
@@ -42,7 +42,7 @@
     sampled_codes,
     levels,
 ):
-    outer, inner, dp = 4, 8, 8
+    outer, inner, dp = 8, 4, 8
     row_count = teacher_hidden.shape[0]
     level_count = teacher_head.shape[1]
     code_count = teacher_head.shape[2]
@@ -51,19 +51,22 @@
     share = student_hidden.shape[1]
     outer_at = lax.axis_index(OUTER)
     inner_at = lax.axis_index(INNER)
-    group_at = outer_at * inner + inner_at
+    group_at = lax.axis_index(GROUP)
 
     def to_gathered(w):
-        return jnp.swapaxes(w.reshape((outer, inner, -1) + w.shape[1:]), 0, 1).reshape(w.shape)
+        parts = w.reshape((outer // 2, inner, 2, -1) + w.shape[1:])
+        return jnp.swapaxes(parts, 0, 1).reshape(w.shape)
 
     def from_gathered(w):
-        return jnp.swapaxes(w.reshape((inner, outer, -1) + w.shape[1:]), 0, 1).reshape(w.shape)
+        parts = w.reshape((inner, outer // 2, 2, -1) + w.shape[1:])
+        return jnp.swapaxes(parts, 0, 1).reshape(w.shape)
 
     teacher_flat = teacher_head.reshape(width_t, level_count * code_count)
     student_flat = student_head.reshape(width_s, level_count * code_count)
     level_mask = (jnp.arange(level_count, dtype=jnp.int32)[:, None] == levels[None, :]).astype(F32)
 
-    teacher_t = spread(spread(teacher_hidden.T, OUTER, outer), INNER, inner)
+    teacher_t = lax.all_gather(teacher_hidden.T, OUTER, axis=0, tiled=True)
+    teacher_t = lax.all_gather(teacher_t, INNER, axis=0, tiled=True)
 
     own_cols = student_hidden.T
     student_t = spread(spread(own_cols, OUTER, outer), INNER, inner)
@@ -144,13 +147,14 @@
     code_part = dot(grad_full, student_centred, 0, 1).astype(BF16)
     back_out = collect(collect(code_part, INNER, inner).astype(BF16), OUTER, outer)
     head_term = dot(normed_out, grad_full, 0, 1).astype(BF16)
-    head_share = collect(head_term, ROWS, dp)
+    head_share = lax.psum_scatter(head_term, ROWS, scatter_dimension=0, tiled=True)
     gained = final_gain * back_out
     back_mixed = (
         scale_out[:, None] * gained
         - mixed_rows * (scale_out**3)[:, None] * jnp.mean(gained * mixed_rows, axis=1)[:, None]
     )
     back_mixed_b = spread(spread(back_mixed.astype(BF16), OUTER, outer), INNER, inner)
+    back_mixed_b, head_share = lax.optimization_barrier((back_mixed_b, head_share))
 
     back_hidden = dot(down_weight, back_mixed_b, 1, 1)
     back_both = jnp.concatenate(
@@ -161,7 +165,9 @@
     )
     both_term = from_gathered(dot(normed_in, back_both, 1, 1).astype(BF16))
     down_term = dot(back_mixed_b, hidden, 0, 1).astype(BF16)
-    grad_share = collect(jnp.concatenate([both_term, down_term], axis=1), ROWS, dp)
+    grad_share = lax.psum_scatter(
+        jnp.concatenate([both_term, down_term], axis=1), ROWS, scatter_dimension=0, tiled=True
+    ).astype(F32)
     gate_share = grad_share[:, :units]
     up_share = grad_share[:, units : 2 * units]
     down_share = grad_share[:, 2 * units :].T
@@ -192,7 +198,7 @@
         + scale_in * own_gain[:, None] * back_in
         - own_cols.astype(F32) * (scale_in**3 * row_mean)
     ).T
-    head_grad = head_share.reshape(head_share.shape[0], level_count, code_count)
+    head_grad = head_share.astype(F32).reshape(head_share.shape[0], level_count, code_count)
     return (token_kl, sampled_score, head_grad, gate_share, up_share, down_share, input_grad)
 
 

time: 457 us -> 404 us (0.88)
  waiting for transfers between devices: 210 us -> 126 us
  blocking collectives: 87.5 us -> 115 us
  between operations: 1.32 us -> 14.5 us
  starting transfers between devices: 53.3 us -> 43.5 us
    all_to_all x6 -> x5, waiting for transfers between devices: 124 us -> 66.1 us  [spread(): got = lax.all_to_all(copies, axes, 0, 0, tiled=True)]
    all_to_all x6 -> x4, waiting for transfers between devices: 85.5 us -> 35.2 us  [collect(): got = lax.all_to_all(parts, axes, 0, 0, tiled=True)]
    all_to_all x2, blocking collectives: 41.5 us -> 77.3 us  [collect(): got = lax.all_to_all(parts, axes, 0, 0, tiled=True)]
    all_gather x0 -> x2, waiting for transfers between devices: none -> 19.7 us  [the longest x1 19.7 us: body(): teacher_t = lax.all_gather(teacher_hidden.T, OUTER, axis=0, tiled=True)]
    all_to_all x6 -> x4, starting transfers between devices: 25.4 us -> 15.8 us  [collect(): got = lax.all_to_all(parts, axes, 0, 0, tiled=True)]
    all_to_all x3 -> x2, blocking collectives: 46 us -> 38.1 us  [spread(): got = lax.all_to_all(copies, axes, 0, 0, tiled=True)]
    broadcast_in_dim x10 -> x8, local copies, waits for them, and re-layouts: 11.1 us -> 7.73 us  [spread(): copies = jnp.broadcast_to(block[None], (count,) + block.shape)]
    all_to_all x6 -> x5, starting transfers between devices: 27.9 us -> 27.4 us  [spread(): got = lax.all_to_all(copies, axes, 0, 0, tiled=True)]
  transfers between devices with their start and end apart: 12 -> 13, of which waited for: 12 -> 11; matrix products, arithmetic and copies ran while one was open for 13% -> 15% of each run, Pallas kernels for 0% -> 0%
where the time goes in v3:
time: 404 us; the launch traced here: 401 us
  waiting for transfers between devices  126 us (31%)
  blocking collectives  115 us (28%)
  starting transfers between devices  43.5 us (11%)
  local copies, waits for them, and re-layouts  40.8 us (10%)
  other arithmetic  38.4 us (10%)
  matrix products  21.7 us (5%)
  between operations  14.5 us (4%)
    all_to_all x2, blocking collectives, collect(): got = lax.all_to_all(parts, axes, 0, 0, tiled=True)  77.3 us
    all_to_all x5, waiting for transfers between devices, spread(): got = lax.all_to_all(copies, axes, 0, 0, tiled=True)  66.1 us
    all_to_all x2, blocking collectives, spread(): got = lax.all_to_all(copies, axes, 0, 0, tiled=True)  38.1 us
    all_to_all x4, waiting for transfers between devices, collect(): got = lax.all_to_all(parts, axes, 0, 0, tiled=True)  35.2 us
    all_to_all x5, starting transfers between devices, spread(): got = lax.all_to_all(copies, axes, 0, 0, tiled=True)  27.4 us
    dot_general x10, matrix products, dot(): lax.dot_general(a, b, (((da,), (db,)), ((), ())), preferred_element_type=...  21.7 us
    all_gather x1, waiting for transfers between devices, body(): teacher_t = lax.all_gather(teacher_hidden.T, OUTER, axis=0, tiled=True)  19.7 us
    unnamed x84, local copies, waits for them, and re-layouts  16.9 us
  transfers between devices with their start and end apart: 13, of which 11 were waited for; matrix products, arithmetic and copies ran while one was open for 15% of the time, Pallas kernels for 0%

profile of v3, /device:TPU:2, one launch (start us, length us, event | category | flops | bytes accessed | tf_op | source)
XLA Modules:
  0.0 400.6 jit_solution(3095497416519085174)
XLA Ops:
  8.9 8.5 %all-to-all-start = ((bf16[8,32,1024]{2,1,0:T(8,128)(2,1)}), bf16[8,32,1024]{2,1,0:T(8,128)(2,1)S(1)}, u32[]{:S(2)}, u32[]{:S(2)}) async-start(bf16[8,32,1024]{2,1,0:T(8,128)(2,1)} %broadcast_in_dim.25), calls=%async_computation | async-start | bytes 1048576 | tf_op jit(solution)/shard_map/all_to_all | solution.py:21
  18.1 16.8 %all-to-all-done = bf16[8,32,1024]{2,1,0:T(8,128)(2,1)S(1)} async-done(((bf16[8,32,1024]{2,1,0:T(8,128)(2,1)}), bf16[8,32,1024]{2,1,0:T(8,128)(2,1)S(1)}, u32[]{:S(2)}, u32[]{:S(2)}) %all-to-all-start) | async-done | bytes 524320 | tf_op jit(solution)/shard_map/all_to_all | solution.py:21
  36.5 4.6 %all-to-all-start.1 = ((bf16[4,256,1024]{2,1,0:T(8,128)(2,1)}), bf16[4,256,1024]{2,1,0:T(8,128)(2,1)S(1)}, u32[]{:S(2)}, u32[]{:S(2)}) async-start(bf16[4,256,1024]{2,1,0:T(8,128)(2,1)} %broadcast_in_dim.27), calls=%async_computation.1 | async-start | bytes 4194304 | tf_op jit(solution)/shard_map/all_to_all | solution.py:21
  41.4 19.7 %all-gather.3.cloned.1.call-done = bf16[640,1024]{1,0:T(8,128)(2,1)} async-done(((bf16[80,1024]{1,0:T(8,128)(2,1)}), bf16[640,1024]{1,0:T(8,128)(2,1)}) %all-gather.3.cloned.1.call-update) | async-done | bytes 1310736 | tf_op jit(solution)/shard_map/all_gather | solution.py:68
  61.1 6.5 %all-to-all-done.1 = bf16[4,256,1024]{2,1,0:T(8,128)(2,1)S(1)} async-done(((bf16[4,256,1024]{2,1,0:T(8,128)(2,1)}), bf16[4,256,1024]{2,1,0:T(8,128)(2,1)S(1)}, u32[]{:S(2)}, u32[]{:S(2)}) %all-to-all-start.1) | async-done | bytes 2097184 | tf_op jit(solution)/shard_map/all_to_all | solution.py:21
  72.0 52.4 %all_to_all.65 = bf16[4,256,1024]{2,1,0:T(8,128)(2,1)} all-to-all(bf16[4,256,1024]{2,1,0:T(8,128)(2,1)S(1)} %bitcast.113), channel_id=1, replica_groups=mesh['zh'=4,'x'=4,'core'=2,'y'=4,'zl'=2] {'y'}, dimensions={0} | all-to-all | bytes 4194304 | tf_op jit(solution)/shard_map/all_to_all | solution.py:27
  136.5 9.7 %all-to-all-done.3 = bf16[8,32,1024]{2,1,0:T(8,128)(2,1)S(1)} async-done(((bf16[8,32,1024]{2,1,0:T(8,128)(2,1)}), bf16[8,32,1024]{2,1,0:T(8,128)(2,1)S(1)}, u32[]{:S(2)}, u32[]{:S(2)}) %all-to-all-start.3) | async-done | bytes 524320 | tf_op jit(solution)/shard_map/all_to_all | solution.py:27
  148.5 22.4 %all_to_all.66 = bf16[8,48,1024]{2,1,0:T(8,128)(2,1)S(1)} all-to-all(bf16[8,48,1024]{2,1,0:T(8,128)(2,1)S(1)} %broadcast_in_dim.28), channel_id=1, replica_groups=mesh['zh'=4,'x'=4,'core'=2,'y'=4,'zl'=2] {'zh','zl'}, dimensions={0} | all-to-all | bytes 1572864 | tf_op jit(solution)/shard_map/all_to_all | solution.py:21
  172.8 4.7 %all-to-all-start.5 = ((bf16[4,272,1024]{2,1,0:T(8,128)(2,1)}), bf16[4,272,1024]{2,1,0:T(8,128)(2,1)}, u32[]{:S(2)}, u32[]{:S(2)}) async-start(bf16[4,272,1024]{2,1,0:T(8,128)(2,1)} %broadcast_in_dim.29), calls=%async_computation.5 | async-start | bytes 4456448 | tf_op jit(solution)/shard_map/all_to_all | solution.py:21
  180.2 6.3 %copy.154 = bf16[2560,3,256]{0,2,1:T(8,128)(2,1)} copy(bf16[2560,3,256]{2,0,1:T(8,128)(2,1)} %param.14) | data formatting | bytes 7864320 | tf_op args[2]
  187.0 13.3 %all-to-all-done.5 = bf16[4,272,1024]{2,1,0:T(8,128)(2,1)} async-done(((bf16[4,272,1024]{2,1,0:T(8,128)(2,1)}), bf16[4,272,1024]{2,1,0:T(8,128)(2,1)}, u32[]{:S(2)}, u32[]{:S(2)}) %all-to-all-start.5) | async-done | bytes 2228256 | tf_op jit(solution)/shard_map/all_to_all | solution.py:21
  214.5 4.2 %fusion.45 = f32[1024,768]{0,1:T(8,128)S(1)} fusion(bf16[2560,768]{0,1:T(8,128)(2,1)S(1)} %bitcast.115, bf16[2560,1024]{1,0:T(8,128)(2,1)S(1)} %bitcast.114), kind=kOutput, calls=%fused_computation.120 | convolution fusion | flops 4026531840 | bytes 12320768 | tf_op jit(solution)/shard_map/dot_general | solution.py:16
  225.9 5.0 %all-to-all-start.6 = ((f32[32,4,1024]{2,1,0:T(4,128)}), f32[32,4,1024]{2,1,0:T(4,128)}, u32[]{:S(2)}, u32[]{:S(2)}) async-start(f32[32,4,1024]{2,1,0:T(4,128)} %broadcast_in_dim.32), calls=%async_computation.6 | async-start | bytes 1048576 | tf_op jit(solution)/shard_map/all_to_all | solution.py:21
  232.5 11.6 %all-to-all-done.6 = f32[32,4,1024]{2,1,0:T(4,128)} async-done(((f32[32,4,1024]{2,1,0:T(4,128)}), f32[32,4,1024]{2,1,0:T(4,128)}, u32[]{:S(2)}, u32[]{:S(2)}) %all-to-all-start.6) | async-done | bytes 524320 | tf_op jit(solution)/shard_map/all_to_all | solution.py:21
  250.6 24.9 %all_to_all.67 = bf16[4,256,1024]{2,1,0:T(8,128)(2,1)} all-to-all(bf16[4,256,1024]{2,1,0:T(8,128)(2,1)S(1)} %bitcast.127), channel_id=1, replica_groups=mesh['zh'=4,'x'=4,'core'=2,'y'=4,'zl'=2] {'y'}, dimensions={0} | all-to-all | bytes 4194304 | tf_op jit(solution)/shard_map/all_to_all | solution.py:27
  278.5 4.1 %all-to-all-start.8 = ((bf16[8,32,1024]{2,1,0:T(8,128)(2,1)}), bf16[8,32,1024]{2,1,0:T(8,128)(2,1)}, u32[]{:S(2)}, u32[]{:S(2)}) async-start(bf16[8,32,1024]{2,1,0:T(8,128)(2,1)} %bitcast.131), calls=%async_computation.8 | async-start | bytes 1048576 | tf_op jit(solution)/shard_map/all_to_all | solution.py:27
  287.3 8.6 %all-to-all-done.8 = bf16[8,32,1024]{2,1,0:T(8,128)(2,1)} async-done(((bf16[8,32,1024]{2,1,0:T(8,128)(2,1)}), bf16[8,32,1024]{2,1,0:T(8,128)(2,1)}, u32[]{:S(2)}, u32[]{:S(2)}) %all-to-all-start.8) | async-done | bytes 524320 | tf_op jit(solution)/shard_map/all_to_all | solution.py:27
  297.3 15.7 %all_to_all.68 = bf16[8,32,1024]{2,1,0:T(8,128)(2,1)S(1)} all-to-all(bf16[8,32,1024]{2,1,0:T(8,128)(2,1)S(1)} %broadcast_in_dim.33), channel_id=1, replica_groups=mesh['zh'=4,'x'=4,'core'=2,'y'=4,'zl'=2] {'zh','zl'}, dimensions={0} | all-to-all | bytes 1048576 | tf_op jit(solution)/shard_map/all_to_all | solution.py:21
  314.7 4.6 %all-to-all-start.10 = ((bf16[4,256,1024]{1,2,0:T(8,128)(2,1)}), bf16[4,256,1024]{1,2,0:T(8,128)(2,1)}, u32[]{:S(2)}, u32[]{:S(2)}) async-start(bf16[4,256,1024]{1,2,0:T(8,128)(2,1)} %broadcast_in_dim.35), calls=%async_computation.10 | async-start | bytes 4194304 | tf_op jit(solution)/shard_map/all_to_all | solution.py:21
  319.5 17.9 %all-to-all-done.10 = bf16[4,256,1024]{1,2,0:T(8,128)(2,1)} async-done(((bf16[4,256,1024]{1,2,0:T(8,128)(2,1)}), bf16[4,256,1024]{1,2,0:T(8,128)(2,1)}, u32[]{:S(2)}, u32[]{:S(2)}) %all-to-all-start.10) | async-done | bytes 2097184 | tf_op jit(solution)/shard_map/all_to_all | solution.py:21
  346.5 4.6 %all-to-all-start.11 = ((bf16[4,272,1024]{2,1,0:T(8,128)(2,1)}), bf16[4,272,1024]{2,1,0:T(8,128)(2,1)}, u32[]{:S(2)}, u32[]{:S(2)}) async-start(bf16[4,272,1024]{2,1,0:T(8,128)(2,1)} %pad_maximum_fusion), calls=%async_computation.13 | async-start | bytes 4456448 | tf_op jit(solution)/shard_map/all_to_all | solution.py:27
  356.4 12.9 %all-to-all-done.11 = bf16[4,272,1024]{2,1,0:T(8,128)(2,1)} async-done(((bf16[4,272,1024]{2,1,0:T(8,128)(2,1)}), bf16[4,272,1024]{2,1,0:T(8,128)(2,1)}, u32[]{:S(2)}, u32[]{:S(2)}) %all-to-all-start.11) | async-done | bytes 2228256 | tf_op jit(solution)/shard_map/all_to_all | solution.py:27
  380.6 4.5 %reduce-scatter.5.cloned.1.call-done = bf16[128,384]{1,0:T(8,128)(2,1)} async-done(((bf16[1024,384]{1,0:T(8,128)(2,1)}), bf16[128,384]{1,0:T(8,128)(2,1)}) %reduce-scatter.5.cloned.1.call-update) | async-done | bytes 98320 | tf_op jit(solution)/shard_map/reduce_scatter | solution.py:168
  388.3 4.1 %all-to-all-done.12 = bf16[8,48,1024]{2,1,0:T(8,128)(2,1)S(1)} async-done(((bf16[8,48,1024]{2,1,0:T(8,128)(2,1)}), bf16[8,48,1024]{2,1,0:T(8,128)(2,1)S(1)}, u32[]{:S(2)}, u32[]{:S(2)}) %all-to-all-start.12) | async-done | bytes 786464 | tf_op jit(solution)/shard_map/all_to_all | solution.py:27
  (194 shorter events, 98.6 us)
Async XLA Ops:
  7.2 64.1 %copy-start = (bf16[128,1024]{1,0:T(8,128)(2,1)S(1)}, bf16[128,1024]{1,0:T(8,128)(2,1)}, u32[]{:S(2)}) copy-start(bf16[128,1024]{1,0:T(8,128)(2,1)} %param.19) | copy-start | bytes 786436
  8.9 26.0 %all-to-all-start = ((bf16[8,32,1024]{2,1,0:T(8,128)(2,1)}), bf16[8,32,1024]{2,1,0:T(8,128)(2,1)S(1)}, u32[]{:S(2)}, u32[]{:S(2)}) async-start(bf16[8,32,1024]{2,1,0:T(8,128)(2,1)} %broadcast_in_dim.25), calls=%async_computation | async-start | bytes 1048576 | tf_op jit(solution)/shard_map/all_to_all | solution.py:21
  17.4 43.7 %all-gather.3.cloned.1.call-start = ((), (), s32[]{:S(2)}) async-start(), calls=%async_computation.15 | async-start | bytes 1474560 | tf_op jit(solution)/shard_map/all_gather | solution.py:68
  36.5 31.1 %all-to-all-start.1 = ((bf16[4,256,1024]{2,1,0:T(8,128)(2,1)}), bf16[4,256,1024]{2,1,0:T(8,128)(2,1)S(1)}, u32[]{:S(2)}, u32[]{:S(2)}) async-start(bf16[4,256,1024]{2,1,0:T(8,128)(2,1)} %broadcast_in_dim.27), calls=%async_computation.1 | async-start | bytes 4194304 | tf_op jit(solution)/shard_map/all_to_all | solution.py:21
  41.1 166.0 %all-gather.5.cloned.1.call-start = ((), (), s32[]{:S(2)}) async-start(), calls=%async_computation.16 | async-start | bytes 6553600 | tf_op jit(solution)/shard_map/all_gather | solution.py:69
  41.2 26.9 %copy-start.22 = (f32[4,4,2,32]{3,2,1,0:T(2,128)}, f32[4,4,2,32]{3,2,1,0:T(2,128)S(1)}, u32[]{:S(2)}) copy-start(f32[4,4,2,32]{3,2,1,0:T(2,128)S(1)} %copy.150) | copy-start | bytes 12292
  41.4 27.3 %copy-start.13 = (bf16[4,4,2,32,256]{4,3,2,1,0:T(8,128)(2,1)}, bf16[4,4,2,32,256]{4,3,2,1,0:T(8,128)(2,1)S(1)}, u32[]{:S(2)}) copy-start(bf16[4,4,2,32,256]{4,3,2,1,0:T(8,128)(2,1)S(1)} %copy.149) | copy-start | bytes 1572868
  127.4 18.8 %all-to-all-start.3 = ((bf16[8,32,1024]{2,1,0:T(8,128)(2,1)}), bf16[8,32,1024]{2,1,0:T(8,128)(2,1)S(1)}, u32[]{:S(2)}, u32[]{:S(2)}) async-start(bf16[8,32,1024]{2,1,0:T(8,128)(2,1)} %bitcast.12), calls=%async_computation.3 | async-start | bytes 1048576 | tf_op jit(solution)/shard_map/all_to_all | solution.py:27
  130.9 17.0 %copy-start.28 = (f32[1024]{0:T(1024)S(1)}, f32[1024]{0:T(1024)}, u32[]{:S(2)}) copy-start(f32[1024]{0:T(1024)} %param.20) | copy-start | bytes 12292
  172.8 27.6 %all-to-all-start.5 = ((bf16[4,272,1024]{2,1,0:T(8,128)(2,1)}), bf16[4,272,1024]{2,1,0:T(8,128)(2,1)}, u32[]{:S(2)}, u32[]{:S(2)}) async-start(bf16[4,272,1024]{2,1,0:T(8,128)(2,1)} %broadcast_in_dim.29), calls=%async_computation.5 | async-start | bytes 4456448 | tf_op jit(solution)/shard_map/all_to_all | solution.py:21
  180.1 6.9 %copy-start.32 = (s32[1024]{0:T(1024)S(1)}, s32[1024]{0:T(1024)}, u32[]{:S(2)}) copy-start(s32[1024]{0:T(1024)} %param.23) | copy-start | bytes 12292
  225.9 18.2 %all-to-all-start.6 = ((f32[32,4,1024]{2,1,0:T(4,128)}), f32[32,4,1024]{2,1,0:T(4,128)}, u32[]{:S(2)}, u32[]{:S(2)}) async-start(f32[32,4,1024]{2,1,0:T(4,128)} %broadcast_in_dim.32), calls=%async_computation.6 | async-start | bytes 1048576 | tf_op jit(solution)/shard_map/all_to_all | solution.py:21
  275.5 7.2 %copy-start.8 = (f32[256,1024]{1,0:T(8,128)S(1)}, f32[256,1024]{1,0:T(8,128)}, u32[]{:S(2)}) copy-start(f32[256,1024]{1,0:T(8,128)} %copy-done.7) | copy-start | bytes 3145732
  278.5 17.4 %all-to-all-start.8 = ((bf16[8,32,1024]{2,1,0:T(8,128)(2,1)}), bf16[8,32,1024]{2,1,0:T(8,128)(2,1)}, u32[]{:S(2)}, u32[]{:S(2)}) async-start(bf16[8,32,1024]{2,1,0:T(8,128)(2,1)} %bitcast.131), calls=%async_computation.8 | async-start | bytes 1048576 | tf_op jit(solution)/shard_map/all_to_all | solution.py:27
  282.6 58.7 %reduce-scatter.3.cloned.1.call-start = ((), (), s32[]{:S(2)}) async-start(), calls=%async_computation.17 | async-start | bytes 1769472 | tf_op jit(solution)/shard_map/reduce_scatter | solution.py:150
  287.3 9.7 %copy-start.29 = (f32[1024]{0:T(1024)S(1)}, f32[1024]{0:T(1024)}, u32[]{:S(2)}) copy-start(f32[1024]{0:T(1024)} %param.20) | copy-start | bytes 12292
  287.3 9.9 %copy-start.35 = (f32[32]{0:T(128)S(1)}, f32[32]{0:T(128)}, u32[]{:S(2)}) copy-start(f32[32]{0:T(128)} %copy-done.34) | copy-start | bytes 388
  287.3 9.9 %copy-start.36 = (f32[32]{0:T(128)S(1)}, f32[32]{0:T(128)}, u32[]{:S(2)}) copy-start(f32[32]{0:T(128)} %get-tuple-element.102) | copy-start | bytes 388
  314.7 22.6 %all-to-all-start.10 = ((bf16[4,256,1024]{1,2,0:T(8,128)(2,1)}), bf16[4,256,1024]{1,2,0:T(8,128)(2,1)}, u32[]{:S(2)}, u32[]{:S(2)}) async-start(bf16[4,256,1024]{1,2,0:T(8,128)(2,1)} %broadcast_in_dim.35), calls=%async_computation.10 | async-start | bytes 4194304 | tf_op jit(solution)/shard_map/all_to_all | solution.py:21
  319.4 21.8 %copy-start.6 = (f32[256,1024]{1,0:T(8,128)S(1)}, f32[256,1024]{1,0:T(8,128)}, u32[]{:S(2)}) copy-start(f32[256,1024]{1,0:T(8,128)} %copy-done.5) | copy-start | bytes 3145732
  346.5 22.8 %all-to-all-start.11 = ((bf16[4,272,1024]{2,1,0:T(8,128)(2,1)}), bf16[4,272,1024]{2,1,0:T(8,128)(2,1)}, u32[]{:S(2)}, u32[]{:S(2)}) async-start(bf16[4,272,1024]{2,1,0:T(8,128)(2,1)} %pad_maximum_fusion), calls=%async_computation.13 | async-start | bytes 4456448 | tf_op jit(solution)/shard_map/all_to_all | solution.py:27
  351.1 34.1 %reduce-scatter.5.cloned.1.call-start = ((), (), s32[]{:S(2)}) async-start(), calls=%async_computation.18 | async-start | bytes 884736 | tf_op jit(solution)/shard_map/reduce_scatter | solution.py:168
  372.7 19.6 %all-to-all-start.12 = ((bf16[8,48,1024]{2,1,0:T(8,128)(2,1)}), bf16[8,48,1024]{2,1,0:T(8,128)(2,1)S(1)}, u32[]{:S(2)}, u32[]{:S(2)}) async-start(bf16[8,48,1024]{2,1,0:T(8,128)(2,1)} %pad_maximum_fusion.2), calls=%async_computation.14 | async-start | bytes 1572864 | tf_op jit(solution)/shard_map/all_to_all | solution.py:27
  379.6 12.9 %copy-start.18 = (bf16[1024,32]{0,1:T(8,128)(2,1)S(1)}, bf16[1024,32]{0,1:T(8,128)(2,1)}, u32[]{:S(2)}) copy-start(bf16[1024,32]{0,1:T(8,128)(2,1)} %param.15) | copy-start | bytes 196612
  (29 other events, 76.5 us)
Sparse Core Ops, SparseCore 0:
  20.0 41.0 all-gather.2
  62.9 80.0 all-gather.4
  287.5 32.2 reduce-scatter.2
  356.5 28.6 reduce-scatter.4
